TPU v7x, 256 devices: a whole 4x4x8 slice. The times are simulated.
256 devices in a mesh: rep: 16 (over x_hi, y, core), fsdp: 16 (over x_lo, z).
Axes of the slice: x: 4 (x_hi: 2, x_lo: 2; x = x_hi * 2 + x_lo), y: 4, z: 8, core: 2. Of those that a mesh axis runs over, the one named last changes fastest.
Arguments:
- features: bfloat16 [16, 8192, 8192], P('rep', 'fsdp'), may hold values from -6 to 6
- targets: bfloat16 [16, 8192, 512], P('rep', 'fsdp'), may hold values from -6 to 6
- value_weight: bfloat16 [16, 8192, 512], P('rep', 'fsdp'), may hold values from -0.0625 to 0.0625
- segment_ids: int32 [16, 8192], P('rep', 'fsdp'), may hold values from -1 to 7, as said below
- traj_counts: int32 [16, 128], P('rep', 'fsdp'), may hold values from 32 to 128
- pseudo_grad: float32 [16, 256, 8192], P('rep', 'fsdp'), may hold values from -6 to 6
- block_exps: int32 [256, 64], P('fsdp'), may hold values from 0 to 3
- outer_params: float32 [256, 8192], P('fsdp'), may hold values from -6 to 6
- outer_moment: float32 [256, 8192], P('fsdp'), may hold values from -3 to 3
Outputs:
- weight_grad: float32 [16, 8192, 512], P('rep', 'fsdp')
- new_params: float32 [256, 8192], P('fsdp')
- new_moment: float32 [256, 8192], P('fsdp')
Inputs may be any that keep to these rules, and one draw needn't show every extreme that they name: `segment_ids`: within each aligned block of 512 tokens the ids start at 0 and never decrease over a live prefix of the block, and are -1 after it; every block has 170 or more live tokens.
All inputs are finite; a program needn't handle non-finite values.
Results may differ from a plain program's by a relative error of at most 0.009.
Values may be sent and summed in bfloat16 or wider, within the bound.
A program may use at most 128 MiB of HBM per device.

v0:
```python
import math

import jax
import jax.numpy as jnp
from jax import lax
from jax.sharding import PartitionSpec as P

BLOCK_WIDTH = 128
SATURATION = 1.0
MOMENTUM = 0.9
OUTER_RATE = 0.7
LOSS_GAIN = 4096.0


def hadamard_table():
    indices = jnp.arange(BLOCK_WIDTH, dtype=jnp.int32)
    masked = jnp.bitwise_and(indices[:, None], indices[None, :])
    parity = jnp.zeros_like(masked)
    for shift in range(7):
        parity = parity + jnp.bitwise_and(jnp.right_shift(masked, shift), 1)
    signs = 1 - 2 * jnp.bitwise_and(parity, 1)
    return signs.astype(jnp.float32) / math.sqrt(BLOCK_WIDTH)


def decode_update(summed, exponents, params, moment, table, replicas):
    rows = summed.shape[0]
    nblocks = summed.shape[1] // BLOCK_WIDTH
    scales = jnp.exp2(exponents.astype(jnp.float32))
    decoded = summed.reshape(rows, nblocks, BLOCK_WIDTH) / replicas * scales[:, :, None]
    delta = jnp.einsum("rbk,kj->rbj", decoded, table, precision=lax.Precision.HIGHEST).reshape(
        rows, nblocks * BLOCK_WIDTH
    )
    new_moment = MOMENTUM * moment + delta
    new_params = params - OUTER_RATE * (delta + MOMENTUM * new_moment)
    return (new_params, new_moment)


def on_device(
    features,
    targets,
    value_weight,
    segment_ids,
    traj_counts,
    pseudo_grad,
    block_exps,
    outer_params,
    outer_moment,
):
    feats = features[0]
    targs = targets[0]
    seg_ids = segment_ids[0]
    counts = traj_counts[0].astype(jnp.float32)
    columns = feats
    predicted = jnp.dot(
        columns,
        lax.all_gather(value_weight[0], "fsdp", axis=0, tiled=True),
        preferred_element_type=jnp.float32,
    )
    live = seg_ids >= 0
    live_total = lax.psum(jnp.sum(live.astype(jnp.float32)), "fsdp")
    slot_range = jnp.arange(counts.shape[0], dtype=jnp.int32)
    onehot = (seg_ids[:, None] == slot_range[None, :]).astype(jnp.float32)
    token_count = jnp.sum(onehot * counts[None, :], axis=1)
    token_count = jnp.where(live, token_count, 1.0)
    errors = predicted - targs.astype(jnp.float32)
    factor = jnp.where(live, LOSS_GAIN / (token_count * live_total), 0.0)
    scaled = (errors * factor[:, None]).astype(jnp.bfloat16)
    columns = feats
    grad_share = lax.psum_scatter(
        lax.dot_general(
            columns, scaled, (((0,), (0,)), ((), ())), preferred_element_type=jnp.float32
        ),
        "fsdp",
        scatter_dimension=0,
        tiled=True,
    )
    weight_grad = grad_share[None]
    table = hadamard_table()
    grad_block = pseudo_grad[0]
    frag_rows = grad_block.shape[0]
    width = grad_block.shape[1]
    nblocks = width // BLOCK_WIDTH
    scales = jnp.exp2(block_exps.astype(jnp.float32))
    rotated = jnp.einsum(
        "rbk,kj->rbj",
        grad_block.reshape(frag_rows, nblocks, BLOCK_WIDTH),
        table,
        precision=lax.Precision.HIGHEST,
    )
    encoded = jnp.clip(rotated / scales[:, :, None], -SATURATION, SATURATION).astype(jnp.bfloat16)
    encoded_wide = encoded.reshape(frag_rows, width).astype(jnp.float32)
    replicas = lax.axis_size("rep")
    summed = lax.psum(encoded_wide.astype(jnp.bfloat16), "rep").astype(jnp.float32)
    new_params, new_moment = decode_update(
        summed, block_exps, outer_params, outer_moment, table, replicas
    )
    return (weight_grad, new_params, new_moment)


def solution(mesh):
    return jax.shard_map(
        on_device,
        mesh=mesh,
        in_specs=(
            P("rep", "fsdp", None),
            P("rep", "fsdp", None),
            P("rep", "fsdp", None),
            P("rep", "fsdp"),
            P("rep", "fsdp"),
            P("rep", "fsdp", None),
            P("fsdp", None),
            P("fsdp", None),
            P("fsdp", None),
        ),
        out_specs=(P("rep", "fsdp", None), P("fsdp", None), P("fsdp", None)),
        check_vma=False,
    )
```

profile of v0, /device:TPU:2, one launch (start us, length us, event | category | flops | bytes accessed | tf_op | source)
XLA Modules:
  0.0 406.9 jit_solution(6655250646262663010)
XLA Ops:
  8.0 0.0 all-gather.3.cloned.1.call-start
  8.0 0.7 all-gather.3.cloned.1.call-update
  8.7 0.0 all-reduce.2.cloned.1.call-start
  8.8 1.1 copy.14
  9.9 0.7 broadcast_multiply_fusion
  10.6 1.3 fusion.21
  12.0 0.0 all-reduce.2.cloned.1.call-update
  12.0 0.0 reduce-scatter.2.cloned.1.call-start
  12.1 1.3 convert_reduce_fusion
  13.3 37.6 %psum.14 = f32[]{:T(128)} all-reduce(f32[]{:T(128)} %get-tuple-element.11), channel_id=1, replica_groups=mesh['rep'=16,'fsdp'=16] {'fsdp'}, use_global_device_ids=true, to_apply=%region_2.0 | all-reduce | flops 1 | bytes 8 | tf_op jit(solution)/shard_map/psum | solution.py:60
  50.9 0.7 convert_bitcast_fusion
  51.6 0.8 select_reduce_fusion
  52.3 0.7 divide_select_fusion
  53.0 61.3 %all-gather.3.cloned.1.call-done = bf16[1,8192,512]{2,1,0:T(8,128)(2,1)} async-done(((bf16[1,512,512]{2,1,0:T(8,128)(2,1)}), bf16[1,8192,512]{2,1,0:T(8,128)(2,1)}) %all-gather.3.cloned.1.call-update) | async-done | bytes 8388624 | tf_op jit(solution)/shard_map/all_gather | solution.py:56
  114.3 10.3 %fusion.14 = bf16[512,512]{1,0:T(8,128)(2,1)S(1)} fusion(bf16[1,8192,512]{2,1,0:T(8,128)(2,1)} %all-gather.3.cloned.1.call-done, bf16[1,512,8192]{2,1,0:T(8,128)(2,1)} %param.9, bf16[1,512,512]{2,1,0:T(8,128)(2,1)} %param.10, f32[512]{0:T(512)S(1)} %divide_select_fusion), kind=kOutput, calls=%fused_computation.7 | convolution fusion | flops 4296015872 | bytes 17827840 | tf_op jit(solution)/shard_map/dot_general | solution.py:54
  124.6 11.6 %convolution_bitcast_fusion = f32[8192,512]{0,1:T(8,128)} fusion(bf16[512,512]{1,0:T(8,128)(2,1)S(1)} %fusion.14, bf16[1,512,8192]{2,1,0:T(8,128)(2,1)} %param.9), kind=kOutput, calls=%fused_computation | convolution fusion | flops 4294967296 | bytes 25690112 | tf_op jit(solution)/shard_map/dot_general | solution.py:70
  136.2 0.0 copy-start
  136.2 0.0 copy-start.1
  136.2 0.0 reduce-scatter.2.cloned.1.call-update
  136.2 257.7 %all-reduce.2.cloned.1.call-done = bf16[16,64,128]{2,1,0:T(8,128)(2,1)} async-done(((bf16[16,64,128]{2,1,0:T(8,128)(2,1)}), bf16[16,64,128]{2,1,0:T(8,128)(2,1)}) %all-reduce.2.cloned.1.call-update) | async-done | bytes 262160 | tf_op jit(solution)/shard_map/psum | solution.py:93
  393.9 1.6 fusion.24
  395.5 0.0 copy-done
  395.5 0.0 copy-done.1
  395.5 1.4 fusion.23
  396.9 0.0 reduce-scatter.2.cloned.1.call-done
  396.9 2.5 copy.13
Async XLA Ops:
  8.0 106.3 %all-gather.3.cloned.1.call-start = ((), (), s32[]{:S(2)}) async-start(), calls=%async_computation.3 | async-start | bytes 8912896 | tf_op jit(solution)/shard_map/all_gather | solution.py:56
  8.7 385.2 %all-reduce.2.cloned.1.call-start = ((), (), s32[]{:S(2)}) async-start(), calls=%async_computation.2 | async-start | bytes 524288 | tf_op jit(solution)/shard_map/psum | solution.py:93
  12.0 384.9 %reduce-scatter.2.cloned.1.call-start = ((), (), s32[]{:S(2)}) async-start(), calls=%async_computation.1 | async-start | bytes 17825792 | tf_op jit(solution)/shard_map/reduce_scatter | solution.py:69
  136.2 259.3 %copy-start = (f32[16,8192]{1,0:T(8,128)S(1)}, f32[16,8192]{1,0:T(8,128)}, u32[]{:S(2)}) copy-start(f32[16,8192]{1,0:T(8,128)} %param.16) | copy-start | bytes 1572868
  136.2 259.3 %copy-start.1 = (f32[16,8192]{1,0:T(8,128)S(1)}, f32[16,8192]{1,0:T(8,128)}, u32[]{:S(2)}) copy-start(f32[16,8192]{1,0:T(8,128)} %param.17) | copy-start | bytes 1572868
Sparse Core Ops, SparseCore 0:
  10.6 103.6 all-gather.2
  136.3 183.2 reduce-scatter.1
Sparse Core Ops, SparseCore 1:
  12.4 381.5 all-reduce.1
where the time goes:
time: 408 us; the launch traced here: 407 us
  waiting for transfers between devices  320 us (78%)
  blocking collectives  37.6 us (9%)
  matrix products  24.8 us (6%)
  between operations  15.5 us (4%)
  other arithmetic  5.44 us (1%)
    psum x1, waiting for transfers between devices, on_device(): lax.psum(encoded_wide.astype(jnp.bfloat16), 'rep').astype(jnp.float32)  258 us
    all_gather x1, waiting for transfers between devices, on_device(): lax.all_gather(value_weight[0], 'fsdp', axis=0, tiled=True)  61.3 us
    psum x1, blocking collectives, on_device(): live_total = lax.psum(jnp.sum(live.astype(jnp.float32)), 'fsdp')  37.6 us
    dot_general x1, matrix products, on_device(): lax.dot_general(columns, scaled, (((0,), (0,)), ((), ())), preferred_elem...  11.6 us
    dot_general x1, matrix products, on_device(): jnp.dot(columns, lax.all_gather(value_weight[0], 'fsdp', axis=0, tiled=Tr...  10.3 us
  transfers between devices with their start and end apart: 3, of which 2 were waited for; matrix products, arithmetic and copies ran while one was open for 8% of the time, Pallas kernels for 0%

commit v1 on v0

v1 whole, which is shorter than its diff:
```python
import functools
import math

import jax
import jax.numpy as jnp
from jax import lax
from jax.experimental import pallas as pl
from jax.experimental.pallas import tpu as pltpu
from jax.sharding import PartitionSpec as P

MESH = pl.DeviceIdType.MESH
BLOCK_WIDTH = 128
MOMENTUM = 0.9
OUTER_RATE = 0.7
LOSS_GAIN = 4096.0
REPLICAS = 16
NZ = 8
BLK = 512
TOK = 512
WIDTH = 8192
COLS = 256
CHUNKS = 2
X_ROWS = 288
X_PART = (128, 160)
ORDER = (4, 3, -3, 2, -2, 1, -1, 0)
F32 = jnp.float32
BF16 = jnp.bfloat16


def sign_table():
    i = lax.broadcasted_iota(jnp.int32, (BLOCK_WIDTH, BLOCK_WIDTH), 0)
    j = lax.broadcasted_iota(jnp.int32, (BLOCK_WIDTH, BLOCK_WIDTH), 1)
    v = jnp.bitwise_and(i, j)
    for shift in (4, 2, 1):
        v = jnp.bitwise_xor(v, jnp.right_shift(v, shift))
    return (1 - 2 * jnp.bitwise_and(v, 1)).astype(F32).astype(BF16)


def rotate(rows, signs):
    hi = rows.astype(BF16)
    rest = rows - hi.astype(F32)
    mid = rest.astype(BF16)
    low = (rest - mid.astype(F32)).astype(BF16)
    total = jnp.dot(low, signs, preferred_element_type=F32)
    total = total + jnp.dot(mid, signs, preferred_element_type=F32)
    total = total + jnp.dot(hi, signs, preferred_element_type=F32)
    return total * (1.0 / math.sqrt(BLOCK_WIDTH))


def kernel(
    feats_hbm, targs_hbm, weight_hbm, seg_ref, counts_ref, pg_hbm, exps_ref, params_hbm, moment_hbm,
    grad_hbm, newp_hbm, newm_hbm,
    feats, targs, wg, acc, st, xs, xr, z0, zr, fxs, fxr, gt, outw,
    cnt_s, cnt_r, pg, scl, enc, enc_r, par_s, par_r, dlt, params, moment,
    load_sem, store_sem, ss, rs,
):
    r, f = lax.axis_index("rep"), lax.axis_index("fsdp")
    x, z = lax.div(f, NZ), lax.rem(f, NZ)
    xh, g = lax.div(r, 8), lax.rem(r, 8)

    def zz(k):
        return lax.rem(z + (k % NZ), NZ)

    def blk(other, k):
        return ((1 - x) if other else x) * NZ + zz(k)

    zdev = {1: (r, blk(0, 1)), -1: (r, blk(0, -1))}
    xdev = (r, blk(1, 0))
    counter = [0]
    pending = []

    def send(src, dst, target):
        i = counter[0]
        counter[0] += 1
        copy = pltpu.make_async_remote_copy(
            src_ref=src, dst_ref=dst, send_sem=ss.at[i], recv_sem=rs.at[i], device_id=target, device_id_type=MESH
        )
        copy.start()
        pending.append(copy)
        return copy

    loads = {}

    def load(name, src, dst):
        loads[name] = pltpu.make_async_copy(src, dst, load_sem.at[len(loads)])
        loads[name].start()

    for c in range(CHUNKS):
        load(f"w{c}", weight_hbm.at[0, :, pl.ds(c * COLS, COLS)], wg.at[c, f])
    load("pg", pg_hbm.at[0], pg)
    load("feats", feats_hbm.at[0], feats)
    load("targs", targs_hbm.at[0], targs)
    load("params", params_hbm, params)
    load("moment", moment_hbm, moment)

    barrier = pltpu.get_barrier_semaphore()
    for k in range(1, 16):
        pl.semaphore_signal(barrier, inc=1, device_id=(r, lax.rem(f + k, 16)), device_id_type=MESH)
    for k in range(1, 8):
        pl.semaphore_signal(barrier, inc=1, device_id=(xh * 8 + lax.rem(g + k, 8), f), device_id_type=MESH)
    pl.semaphore_signal(barrier, inc=1, device_id=((1 - xh) * 8 + g, f), device_id_type=MESH)

    seg = seg_ref[...]
    live = seg >= 0
    live_here = jnp.sum(live.astype(F32), axis=1, keepdims=True)
    cnt_s[...] = jnp.broadcast_to(live_here, (8, 128))
    tok_count = jnp.zeros((1, TOK), F32)
    counts = counts_ref[...].astype(F32)
    for s in range(8):
        tok_count = tok_count + jnp.where(seg == s, counts[:, s : s + 1], 0.0)
    tok_count = jnp.where(live, tok_count, 1.0)
    pl.semaphore_wait(barrier, 23)

    class Gather:
        def __init__(self, c):
            self.c = c
            self.got = {}
            self.xgot = {}

        def rows(self, j, lo, n):
            return self.ref(j).at[pl.ds(lo, n)]

        def ref(self, j):
            return wg.at[self.c, j]

        def push(self, j, lo, n, target):
            ref = self.rows(j, lo, n)
            return send(ref, ref, target)

        def start(self):
            loads[f"w{self.c}"].wait()
            own = blk(0, 0)
            self.nb = self.push(own, X_ROWS, BLK - X_ROWS, xdev)
            for d in (1, -1):
                self.got[d, 1, "o"] = self.push(own, X_ROWS, BLK - X_ROWS, zdev[d])
            for d in (1, -1):
                self.got[d, 1, "x"] = self.push(own, 0, X_ROWS, zdev[d])
            self.xgot[0] = [self.push(own, 0, X_ROWS, xdev)]

        def cross(self):
            self.nb.wait_recv()
            for d in (1, -1):
                self.got[d, 1, "n"] = self.push(blk(1, 0), X_ROWS, BLK - X_ROWS, zdev[d])

        def step(self, s):
            for name in ("o", "x", "n"):
                for d in (1, -1):
                    self.got[d, s, name].wait_recv()
                    j = blk(name == "n", -d * s)
                    lo, n = (0, X_ROWS) if name == "x" else (X_ROWS, BLK - X_ROWS)
                    hlo, hn = (lo, n // 2) if d == 1 else (lo + n // 2, n // 2)
                    if s < 3:
                        self.got[d, s + 1, name] = self.push(j, lo, n, zdev[d])
                    elif s == 3:
                        self.got[d, s + 1, name] = self.push(j, hlo, hn, zdev[d])
                    if name == "x":
                        flo, fn = (lo, n) if s < 4 else (hlo, hn)
                        key = -d * s if s < 4 else 4
                        self.xgot.setdefault(key, []).append(self.push(j, flo, fn, xdev))

        def product(self, k):
            c = self.c
            total = None
            for kk in ((0,) if k == 0 else (4,) if k == 4 else (k, -k)):
                for copy in self.xgot[kk]:
                    copy.wait_recv()
                for other in (0, 1):
                    j = blk(other, kk)
                    cols = pl.ds(pl.multiple_of(j * BLK, BLK), BLK)
                    part = jnp.dot(feats[:, cols], wg[c, j], preferred_element_type=F32)
                    if k == 0 and total is None:
                        acc[c] = part
                    else:
                        acc[c] += part
                    total = 0

    def scaled(c):
        err = acc[c] - targs[:, c * COLS : (c + 1) * COLS].astype(F32)
        st[c] = (err.T * factor_row()).astype(BF16)

    factor_cache = []

    def factor_row():
        if not factor_cache:
            for copy in counted:
                copy.wait_recv()
            total = live_here
            for k in range(1, 16):
                total = total + cnt_r[k][0:1, 0:1]
            factor_cache.append(jnp.where(live, LOSS_GAIN / (tok_count * total), 0.0))
        return factor_cache[0]

    class Scatter:
        def __init__(self, c):
            self.c = c
            self.nx = X_PART[c]
            self.got = {}
            self.xgot = {}

        def span(self, name):
            return (0, self.nx) if name == "x" else (self.nx, COLS - self.nx)

        def half(self, name, d):
            lo, n = self.span(name)
            return (lo, n // 2) if d == 1 else (lo + n // 2, n // 2)

        def dot(self, other, k, lo, n):
            cols = pl.ds(pl.multiple_of(blk(other, k) * BLK, BLK), BLK)
            return jnp.dot(st[self.c, lo : lo + n], feats[:, cols], preferred_element_type=F32)

        def cross(self, ki):
            c, k = self.c, ORDER[ki]
            lo, n = self.span("x")
            xs[c, ki, 0:n] = self.dot(1, k, lo, n).astype(BF16)
            self.xgot[k] = send(xs.at[c, ki, pl.ds(0, n)], xr.at[c, ki, pl.ds(0, n)], xdev)

        def first(self, names):
            c = self.c
            for name in names:
                lo, n = self.span(name)
                col = 1 if name == "n" else 0
                val = self.dot(col, 4, lo, n)
                if name == "x":
                    self.xgot[4].wait_recv()
                    val = val + xr[c, 0, 0:n].astype(F32)
                z0[c, col, lo : lo + n] = val.astype(BF16)
                for d in (1, -1):
                    hlo, hn = self.half(name, d)
                    self.got[d, 1, name] = send(
                        z0.at[c, col, pl.ds(hlo, hn)], zr.at[c, (1 - d) // 2, 0, col, pl.ds(hlo, hn)], zdev[d]
                    )

        def step(self, s, names=("o", "n", "x")):
            c = self.c
            for name in names:
                lo, n = self.span(name)
                col = 1 if name == "n" else 0
                for d in (1, -1):
                    di = (1 - d) // 2
                    gt[di, lo : lo + n] = self.dot(col, d * (4 - s), lo, n)
                for d in (1, -1):
                    di = (1 - d) // 2
                    k = d * (4 - s)
                    ki = ORDER.index(k)
                    if name == "x":
                        self.xgot[k].wait_recv()
                    self.got[d, s, name].wait_recv()
                    for part in (1, -1):
                        plo, pn = self.half(name, part)
                        val = gt[di, plo : plo + pn]
                        if name == "x":
                            val = val + xr[c, ki, plo : plo + pn].astype(F32)
                        if s > 1 or part == d:
                            val = val + zr[c, di, s - 1, col, plo : plo + pn].astype(F32)
                        zr[c, di, s - 1, col, plo : plo + pn] = val.astype(BF16)
                    self.got[d, s + 1, name] = send(
                        zr.at[c, di, s - 1, col, pl.ds(lo, n)], zr.at[c, di, s, col, pl.ds(lo, n)], zdev[d]
                    )

        def arrived(self, name):
            c = self.c
            lo, n = self.span(name)
            col = 1 if name == "n" else 0
            val = self.dot(col, 0, lo, n)
            if name == "x":
                self.xgot[0].wait_recv()
                val = val + xr[c, ORDER.index(0), 0:n].astype(F32)
            for d in (1, -1):
                self.got[d, 4, name].wait_recv()
                val = val + zr[c, (1 - d) // 2, 3, col, lo : lo + n].astype(F32)
            return val

        def last(self):
            c = self.c
            lo, n = self.span("n")
            fxs[c, 0:n] = self.arrived("n").astype(BF16)
            copy = send(fxs.at[c, pl.ds(0, n)], fxr.at[c, pl.ds(0, n)], xdev)
            gt[0, lo : lo + n] = self.arrived("o")
            gt[0, 0 : self.nx] = self.arrived("x")
            copy.wait_recv()
            gt[0, lo : lo + n] += fxr[c, 0:n].astype(F32)
            outw[c] = gt[0].T
            store(outw.at[c], grad_hbm.at[0, :, pl.ds(c * COLS, COLS)])

    stores = []

    def store(src, dst):
        copy = pltpu.make_async_copy(src, dst, store_sem.at[len(stores)])
        copy.start()
        stores.append(copy)

    nb8 = WIDTH // 8 // BLOCK_WIDTH

    def encode():
        loads["pg"].wait()
        signs = sign_table()
        inv = jnp.right_shift(8, exps_ref[...]).astype(F32) * 0.125
        scale = jnp.left_shift(1, exps_ref[...]).astype(F32)
        for p in range(8):
            base = p * nb8
            rows = jnp.concatenate(
                [pg[:, (base + b) * BLOCK_WIDTH : (base + b + 1) * BLOCK_WIDTH] for b in range(nb8)], axis=0
            )
            turned = rotate(rows, signs)
            for b in range(nb8):
                at = slice(b * BLOCK_WIDTH, (b + 1) * BLOCK_WIDTH)
                val = turned[b * 16 : (b + 1) * 16] * inv[:, base + b : base + b + 1]
                enc[p, :, at] = jnp.clip(val, -1.0, 1.0).astype(BF16)
                scl[p, :, at] = jnp.broadcast_to(scale[:, base + b : base + b + 1], (16, BLOCK_WIDTH))
        out = []
        for k in range(1, 8):
            p = lax.rem(g + k, 8)
            out.append(send(enc.at[p], enc_r.at[k - 1], (xh * 8 + p, f)))
        return out

    def partial_sum(sent):
        total = enc[g].astype(F32)
        for k in range(1, 8):
            sent[k - 1].wait_recv()
            total = total + enc_r[k - 1].astype(F32)
        par_s[...] = total.astype(BF16)
        return send(par_s, par_r, ((1 - xh) * 8 + g, f))

    def decode(sent):
        sent.wait_recv()
        val = (par_s[...].astype(F32) + par_r[...].astype(F32)) * (1.0 / REPLICAS) * scl[g]
        rows = jnp.concatenate([val[:, b * BLOCK_WIDTH : (b + 1) * BLOCK_WIDTH] for b in range(nb8)], axis=0)
        turned = rotate(rows, sign_table()).astype(BF16)
        for b in range(nb8):
            dlt[g, :, b * BLOCK_WIDTH : (b + 1) * BLOCK_WIDTH] = turned[b * 16 : (b + 1) * 16]
        out = []
        for k in range(1, 8):
            p = lax.rem(g + k, 8)
            out.append(send(dlt.at[g], dlt.at[g], (xh * 8 + p, f)))
        return out

    def update(sent):
        for copy in sent:
            copy.wait_recv()
        loads["params"].wait()
        loads["moment"].wait()
        for p in range(8):
            at = slice(p * 1024, (p + 1) * 1024)
            delta = dlt[p].astype(F32)
            new = MOMENTUM * moment[:, at] + delta
            moment[:, at] = new
            params[:, at] = params[:, at] - OUTER_RATE * (delta + MOMENTUM * new)
        store(params, newp_hbm)
        store(moment, newm_hbm)

    g0, g1 = Gather(0), Gather(1)
    s0, s1 = Scatter(0), Scatter(1)
    g0.start()
    counted = [send(cnt_s, cnt_r.at[k], (r, lax.rem(f + k, 16))) for k in range(1, 16)]
    g0.cross()
    sent = encode()
    g0.step(1)
    loads["feats"].wait()
    g0.product(0)
    sent = partial_sum(sent)
    g0.step(2)
    g0.product(1)
    sent = decode(sent)
    g0.step(3)
    g1.start()
    g0.product(2)
    g1.cross()
    g0.step(4)
    update(sent)
    g1.step(1)
    g0.product(3)
    g0.product(4)
    loads["targs"].wait()
    scaled(0)
    g1.product(0)
    g1.step(2)
    g1.product(1)
    s0.cross(0)
    g1.step(3)
    s0.first(("o", "n"))
    g1.product(2)
    s0.cross(1)
    s0.cross(2)
    g1.step(4)
    s0.first(("x",))
    for ki in range(3, 8):
        s0.cross(ki)
    s0.step(1)
    g1.product(3)
    g1.product(4)
    scaled(1)
    s0.step(2)
    for ki in range(0, 8):
        s1.cross(ki)
    s1.first(("o", "n"))
    s0.step(3)
    s1.first(("x",))
    s1.step(1)
    s0.last()
    s1.step(2)
    s1.step(3)
    s1.last()

    for copy in pending:
        copy.wait_send()
    for copy in stores:
        copy.wait()


def on_device(features, targets, value_weight, segment_ids, traj_counts, pseudo_grad, block_exps, outer_params, outer_moment):
    hbm = pl.BlockSpec(memory_space=pl.ANY)
    vmem = pl.BlockSpec(memory_space=pltpu.VMEM)
    xmax = max(X_PART)
    zmax = COLS - min(X_PART)
    n_sem = 256
    out = pl.pallas_call(
        kernel,
        out_shape=(
            jax.ShapeDtypeStruct((1, BLK, 2 * COLS), F32),
            jax.ShapeDtypeStruct((16, WIDTH), F32),
            jax.ShapeDtypeStruct((16, WIDTH), F32),
        ),
        in_specs=[hbm, hbm, hbm, vmem, vmem, hbm, vmem, hbm, hbm],
        out_specs=(hbm, hbm, hbm),
        scratch_shapes=[
            pltpu.VMEM((TOK, WIDTH), BF16),
            pltpu.VMEM((TOK, 2 * COLS), BF16),
            pltpu.VMEM((CHUNKS, 16, BLK, COLS), BF16),
            pltpu.VMEM((CHUNKS, TOK, COLS), F32),
            pltpu.VMEM((CHUNKS, COLS, TOK), BF16),
            pltpu.VMEM((CHUNKS, 8, xmax, BLK), BF16),
            pltpu.VMEM((CHUNKS, 8, xmax, BLK), BF16),
            pltpu.VMEM((CHUNKS, 2, COLS, BLK), BF16),
            pltpu.VMEM((CHUNKS, 2, 4, 2, COLS, BLK), BF16),
            pltpu.VMEM((CHUNKS, zmax, BLK), BF16),
            pltpu.VMEM((CHUNKS, zmax, BLK), BF16),
            pltpu.VMEM((2, COLS, BLK), F32),
            pltpu.VMEM((CHUNKS, BLK, COLS), F32),
            pltpu.VMEM((8, 128), F32),
            pltpu.VMEM((16, 8, 128), F32),
            pltpu.VMEM((16, WIDTH), F32),
            pltpu.VMEM((8, 16, 1024), F32),
            pltpu.VMEM((8, 16, 1024), BF16),
            pltpu.VMEM((7, 16, 1024), BF16),
            pltpu.VMEM((16, 1024), BF16),
            pltpu.VMEM((16, 1024), BF16),
            pltpu.VMEM((8, 16, 1024), BF16),
            pltpu.VMEM((16, WIDTH), F32),
            pltpu.VMEM((16, WIDTH), F32),
            pltpu.SemaphoreType.DMA((8,)),
            pltpu.SemaphoreType.DMA((8,)),
            pltpu.SemaphoreType.DMA((n_sem,)),
            pltpu.SemaphoreType.DMA((n_sem,)),
        ],
        compiler_params=pltpu.CompilerParams(
            collective_id=0, has_side_effects=True, vmem_limit_bytes=56 * 2**20
        ),
    )(features, targets, value_weight, segment_ids, traj_counts, pseudo_grad, block_exps, outer_params, outer_moment)
    return out


def solution(mesh):
    return jax.shard_map(
        on_device,
        mesh=mesh,
        in_specs=(
            P("rep", "fsdp", None),
            P("rep", "fsdp", None),
            P("rep", "fsdp", None),
            P("rep", "fsdp"),
            P("rep", "fsdp"),
            P("rep", "fsdp", None),
            P("fsdp", None),
            P("fsdp", None),
            P("fsdp", None),
        ),
        out_specs=(P("rep", "fsdp", None), P("fsdp", None), P("fsdp", None)),
        check_vma=False,
    )
```

time: 408 us -> 157 us (0.38)
  waiting for transfers between devices: 320 us -> 0 us
  Pallas kernels: 0 us -> 150 us
  blocking collectives: 37.6 us -> 0 us
  matrix products: 24.8 us -> 0 us
  between operations: 15.5 us -> 0.64 us
  other arithmetic: 5.44 us -> 0 us
    psum x1 -> x0, waiting for transfers between devices: 258 us -> none  [on_device(): lax.psum(encoded_wide.astype(jnp.bfloat16), 'rep').astype(jnp.float32)]
    pallas_call x0 -> x1, Pallas kernels: none -> 150 us  [on_device(): pl.pallas_call(kernel, out_shape=(jax.ShapeDtypeStruct((1, BLK, 2 * COLS)...]
    all_gather x1 -> x0, waiting for transfers between devices: 61.3 us -> none  [on_device(): lax.all_gather(value_weight[0], 'fsdp', axis=0, tiled=True)]
    psum x1 -> x0, blocking collectives: 37.6 us -> none  [on_device(): live_total = lax.psum(jnp.sum(live.astype(jnp.float32)), 'fsdp')]
    dot_general x4 -> x0, matrix products: 24.8 us -> none  [the longest x1 11.6 us: on_device(): lax.dot_general(columns, scaled, (((0,), (0,)), ((), ())), preferred_elem...]
  transfers between devices with their start and end apart: 3 -> 0, of which waited for: 2 -> 0; matrix products, arithmetic and copies ran while one was open for 8% -> 0% of each run, Pallas kernels for 0% -> 0%
where the time goes in v1:
time: 157 us
  Pallas kernels  150 us (96%)
  local copies, waits for them, and re-layouts  6 us (4%)
    pallas_call x1, Pallas kernels, on_device(): pl.pallas_call(kernel, out_shape=(jax.ShapeDtypeStruct((1, BLK, 2 * COLS)...  150 us
    unnamed x3, local copies, waits for them, and re-layouts  6 us

profile of v1, /device:TPU:2, one launch (start us, length us, event | category | flops | bytes accessed | tf_op | source)
XLA Modules:
  0.0 156.8 jit_solution(15456862778189712494)
XLA Ops:
  0.6 150.1 %shard_map.112 = (f32[1,512,512]{2,1,0:T(8,128)}, f32[16,8192]{1,0:T(8,128)}, f32[16,8192]{1,0:T(8,128)}) custom-call(bf16[1,512,8192]{2,1,0:T(8,128)(2,1)} %feats_hbm.1, bf16[1,512,512]{2,1,0:T(8,128)(2,1)} %targs_hbm.1, bf16[1,512,512]{2,1,0:T(8,128)(2,1)} %weight_hbm.1, s32[1,512]{1,0:T(1,128)} %seg_ref.1, s32[1,8]{1,0:T(1,128)} %counts_ref.1, ...), custom_call_target="tpu_custom_call" | custom-call | tf_op jit(solution)/shard_map/pallas_call | solution.py:416
  150.8 2.3 %copy.15 = f32[1,512,512]{2,1,0:T(8,128)} copy(f32[1,512,512]{2,1,0:T(8,128)} %get-tuple-element.6) | data formatting | bytes 2097152
  153.0 1.9 %copy.16 = f32[16,8192]{1,0:T(8,128)} copy(f32[16,8192]{1,0:T(8,128)} %get-tuple-element.7) | data formatting | bytes 1048576
  154.9 1.9 %copy.17 = f32[16,8192]{1,0:T(8,128)} copy(f32[16,8192]{1,0:T(8,128)} %get-tuple-element.8) | data formatting | bytes 1048576

commit v2 on v0

v2 whole, which is shorter than its diff:
```python
import functools
import math

import jax
import jax.numpy as jnp
from jax import lax
from jax.experimental import pallas as pl
from jax.experimental.pallas import tpu as pltpu
from jax.sharding import PartitionSpec as P

MESH = pl.DeviceIdType.MESH
BLOCK_WIDTH = 128
MOMENTUM = 0.9
OUTER_RATE = 0.7
LOSS_GAIN = 4096.0
REPLICAS = 16
NZ = 8
BLK = 512
TOK = 512
WIDTH = 8192
COLS = 256
CHUNKS = 2
N_SLOTS = 123
EXTRA = 32
X_ROWS = (320, 192)
X_PART = (160, 160)
ORDER = (4, 3, -3, 2, -2, 1, -1, 0)
F32 = jnp.float32
BF16 = jnp.bfloat16
PLAN = (
    ("gs", 0), ("gc", 0), ("gf", 0, 1, "o", 1), ("gf", 0, 1, "o", -1),
    ("enc",), ("gp", 0, 0), ("gf", 0, 1, "x", 1), ("gf", 0, 1, "x", -1),
    ("gf", 0, 1, "n", 1), ("gf", 0, 1, "n", -1), ("par",), ("gf", 0, 2, "o", 1),
    ("gf", 0, 2, "o", -1), ("gf", 0, 2, "x", 1), ("gf", 0, 2, "x", -1), ("gp", 0, 1),
    ("gf", 0, 2, "n", 1), ("gf", 0, 2, "n", -1), ("dec",), ("gf", 0, 3, "o", 1),
    ("gf", 0, 3, "o", -1), ("gf", 0, 3, "x", 1), ("gf", 0, 3, "x", -1), ("upd",),
    ("gp", 0, 2), ("gf", 0, 3, "n", 1), ("gf", 0, 3, "n", -1), ("gs", 1),
    ("gf", 0, 4, "o", 1), ("gf", 0, 4, "o", -1), ("gf", 0, 4, "x", 1), ("gf", 0, 4, "x", -1),
    ("gf", 0, 4, "n", 1), ("gf", 0, 4, "n", -1), ("gp", 0, 3), ("gf", 1, 1, "o", 1),
    ("gf", 1, 1, "o", -1), ("gf", 1, 1, "x", 1), ("gf", 1, 1, "x", -1), ("gc", 1),
    ("gp", 1, 0), ("gf", 1, 2, "o", 1), ("gf", 1, 2, "o", -1), ("gf", 1, 2, "x", 1),
    ("gf", 1, 2, "x", -1), ("gp", 0, 4), ("sc", 0), ("gf", 1, 1, "n", 1),
    ("gf", 1, 1, "n", -1), ("gp", 1, 1), ("rc", 0, 0), ("gf", 1, 3, "o", 1),
    ("gf", 1, 3, "o", -1), ("gf", 1, 3, "x", 1), ("gf", 1, 3, "x", -1), ("rf", 0, "o"),
    ("gf", 1, 2, "n", 1), ("gf", 1, 2, "n", -1), ("gp", 1, 2), ("rc", 0, 1),
    ("gf", 1, 4, "o", 1), ("gf", 1, 4, "o", -1), ("gf", 1, 4, "x", 1), ("gf", 1, 4, "x", -1),
    ("rs", 0, 1, "o", 1), ("rs", 0, 1, "o", -1), ("rf", 0, "n"), ("rc", 0, 2),
    ("gf", 1, 3, "n", 1), ("gf", 1, 3, "n", -1), ("gp", 1, 3), ("rf", 0, "x"),
    ("rs", 0, 2, "o", 1), ("rs", 0, 2, "o", -1), ("rc", 0, 3), ("rs", 0, 1, "n", 1),
    ("rs", 0, 1, "n", -1), ("gf", 1, 4, "n", 1), ("gf", 1, 4, "n", -1), ("gp", 1, 4),
    ("sc", 1), ("rc", 0, 4), ("rs", 0, 1, "x", 1), ("rs", 0, 1, "x", -1),
    ("rs", 0, 3, "o", 1), ("rs", 0, 3, "o", -1), ("rc", 0, 5), ("rs", 0, 2, "n", 1),
    ("rs", 0, 2, "n", -1), ("rc", 0, 6), ("rs", 0, 2, "x", 1), ("rs", 0, 2, "x", -1),
    ("rl", 0, "o"), ("rc", 0, 7), ("rs", 0, 3, "n", 1), ("rs", 0, 3, "n", -1),
    ("rc", 1, 0), ("rf", 1, "o"), ("rs", 0, 3, "x", 1), ("rs", 0, 3, "x", -1),
    ("rc", 1, 1), ("rl", 0, "n"), ("rs", 1, 1, "o", 1), ("rs", 1, 1, "o", -1),
    ("rf", 1, "n"), ("rf", 1, "x"), ("rl", 0, "x"), ("rc", 1, 2),
    ("rs", 1, 2, "o", 1), ("rs", 1, 2, "o", -1), ("rs", 1, 1, "n", 1), ("rs", 1, 1, "n", -1),
    ("fin", 0), ("rc", 1, 3), ("rs", 1, 1, "x", 1), ("rs", 1, 3, "o", 1),
    ("rs", 1, 3, "o", -1), ("rs", 1, 1, "x", -1), ("rc", 1, 4), ("rs", 1, 2, "n", 1),
    ("rs", 1, 2, "n", -1), ("rc", 1, 5), ("rs", 1, 2, "x", 1), ("rl", 1, "o"),
    ("rc", 1, 6), ("rs", 1, 2, "x", -1), ("rs", 1, 3, "n", 1), ("rs", 1, 3, "n", -1),
    ("rc", 1, 7), ("rs", 1, 3, "x", 1), ("rs", 1, 3, "x", -1), ("rl", 1, "n"),
    ("rl", 1, "x"), ("fin", 1),
)


def sign_table():
    i = lax.broadcasted_iota(jnp.int32, (BLOCK_WIDTH, BLOCK_WIDTH), 0)
    j = lax.broadcasted_iota(jnp.int32, (BLOCK_WIDTH, BLOCK_WIDTH), 1)
    v = jnp.bitwise_and(i, j)
    for shift in (4, 2, 1):
        v = jnp.bitwise_xor(v, jnp.right_shift(v, shift))
    return (1 - 2 * jnp.bitwise_and(v, 1)).astype(F32).astype(BF16)


def rotate(rows, signs):
    hi = rows.astype(BF16)
    rest = rows - hi.astype(F32)
    mid = rest.astype(BF16)
    low = (rest - mid.astype(F32)).astype(BF16)
    total = jnp.dot(low, signs, preferred_element_type=F32)
    total = total + jnp.dot(mid, signs, preferred_element_type=F32)
    total = total + jnp.dot(hi, signs, preferred_element_type=F32)
    return total * (1.0 / math.sqrt(BLOCK_WIDTH))


def kernel(
    feats_hbm, targs_hbm, weight_hbm, seg_hbm, counts_hbm, pg_hbm, exps_hbm,
    grad_hbm, delta_hbm,
    feats, targs, wg, acc, st, xs, xr, z0, zr, fxs, fxr, gt, outw,
    pg, scl, enc, landed, par_s, dlt,
    seg_ref, counts_ref, exps_ref, load_sem, store_sem, ss, rs,
):
    r, f = lax.axis_index("rep"), lax.axis_index("fsdp")
    x, z = lax.div(f, NZ), lax.rem(f, NZ)
    xh, g = lax.div(r, 8), lax.rem(r, 8)

    def zz(k):
        return lax.rem(z + (k % NZ), NZ)

    def blk(other, k):
        return ((1 - x) if other else x) * NZ + zz(k)

    zdev = {1: (r, blk(0, 1)), -1: (r, blk(0, -1))}
    xdev = (r, blk(1, 0))
    slots = {}

    def slot(key):
        return rs.at[slots.setdefault(key, len(slots))]

    def send(key, src, dst, target, group):
        pltpu.make_async_remote_copy(
            src_ref=src, dst_ref=dst, send_sem=ss.at[group], recv_sem=slot(key), device_id=target, device_id_type=MESH
        ).start()

    def arrive(key, ref):
        pltpu.make_async_copy(ref, ref, slot(key)).wait()

    def sent(group, ref):
        pltpu.make_async_copy(ref, ref, ss.at[group]).wait()

    loads = {}

    def load(name, src, dst):
        loads[name] = pltpu.make_async_copy(src, dst, load_sem.at[len(loads)])
        loads[name].start()

    for c in range(CHUNKS):
        load(f"w{c}", weight_hbm.at[0, :, pl.ds(c * COLS, COLS)], wg.at[c, f, pl.ds(0, BLK)])
    load("seg", seg_hbm, seg_ref)
    load("counts", counts_hbm, counts_ref)
    load("exps", exps_hbm, exps_ref)
    load("pg", pg_hbm.at[0], pg)
    load("feats", feats_hbm.at[0], feats)
    load("targs", targs_hbm.at[0], targs)

    barrier = pltpu.get_barrier_semaphore()
    for target in (zdev[1], zdev[-1], xdev):
        pl.semaphore_signal(barrier, inc=1, device_id=target, device_id_type=MESH)
    for k in range(1, 8):
        pl.semaphore_signal(barrier, inc=1, device_id=(xh * 8 + lax.rem(g + k, 8), f), device_id_type=MESH)
    pl.semaphore_signal(barrier, inc=1, device_id=((1 - xh) * 8 + g, f), device_id_type=MESH)

    loads["seg"].wait()
    loads["counts"].wait()
    seg = seg_ref[...]
    live = seg >= 0
    live_here = jnp.sum(live.astype(F32), axis=1, keepdims=True)
    tens = jnp.floor(live_here * (1.0 / 16))
    wg[0, f, BLK:, 0:128] = jnp.broadcast_to(tens, (EXTRA, 128)).astype(BF16)
    wg[0, f, BLK:, 128:] = jnp.broadcast_to(live_here - 16 * tens, (EXTRA, COLS - 128)).astype(BF16)
    tok_count = jnp.zeros((1, TOK), F32)
    counts = counts_ref[...].astype(F32)
    for s in range(8):
        tok_count = tok_count + jnp.where(seg == s, counts[:, s : s + 1], 0.0)
    tok_count = jnp.where(live, tok_count, 1.0)
    pl.semaphore_wait(barrier, 11)

    def gather_push(key, c, j, lo, n, target):
        ref = wg.at[c, j, pl.ds(lo, n)]
        send(key, ref, ref, target, c)

    def gather_span(c, name):
        return (0, X_ROWS[c]) if name == "x" else (X_ROWS[c], BLK - X_ROWS[c] + (0 if c else EXTRA))

    def part_of(lo, n, d):
        return (lo, n // 2) if d == 1 else (lo + n // 2, n // 2)

    def gather_start(c):
        loads[f"w{c}"].wait()
        own = blk(0, 0)
        lo, n = gather_span(c, "o")
        if n:
            gather_push(("nb", c), c, own, lo, n, xdev)
        for name in ("o", "x"):
            lo, n = gather_span(c, name)
            if n:
                for d in (1, -1):
                    gather_push(("g", c, d, 1, name), c, own, lo, n, zdev[d])
        if n:
            gather_push(("gx", c, 0), c, own, lo, n, xdev)

    def gather_cross(c):
        lo, n = gather_span(c, "n")
        arrive(("nb", c), wg.at[c, blk(1, 0), pl.ds(lo, n)])
        for d in (1, -1):
            gather_push(("g", c, d, 1, "n"), c, blk(1, 0), lo, n, zdev[d])

    def gather_forward(c, s, name, d):
        j = blk(name == "n", -d * s)
        lo, n = gather_span(c, name)
        half = part_of(lo, n, d)
        arrive(("g", c, d, s, name), wg.at[c, j, pl.ds(*((lo, n) if s < 4 else half))])
        if s < 4:
            at = (lo, n) if s < 3 else half
            gather_push(("g", c, d, s + 1, name), c, j, *at, zdev[d])
        if name == "x":
            at = (lo, n) if s < 4 else half
            gather_push(("gx", c, s), c, j, *at, xdev)

    def product(c, k):
        if k == 0:
            loads_once("feats")
        if X_ROWS[c]:
            lo, n = gather_span(c, "x")
            if k in (0, 4):
                arrive(("gx", c, k), wg.at[c, blk(1, k), pl.ds(lo, n)])
            else:
                arrive(("gx", c, k), wg.at[c, pl.ds(0, 2), pl.ds(lo, n)])
        for kk in (k,) if k in (0, 4) else (k, -k):
            for other in (0, 1):
                j = blk(other, kk)
                cols = pl.ds(pl.multiple_of(j * BLK, BLK), BLK)
                part = jnp.dot(feats[:, cols], wg[c, j, 0:BLK], preferred_element_type=F32)
                if (kk, other) == (0, 0):
                    acc[c] = part
                else:
                    acc[c] += part

    waited = set()

    def loads_once(name):
        if name not in waited:
            waited.add(name)
            loads[name].wait()

    factor_cache = []

    def factor_row():
        if not factor_cache:
            total = jnp.zeros((1, 1), F32)
            for j in range(16):
                digits = wg[0, j, BLK : BLK + 16].astype(F32)
                total = total + (16 * digits[0:1, 0:1] + digits[0:1, 128:129])
            factor_cache.append(jnp.where(live, LOSS_GAIN / (tok_count * total), 0.0))
        return factor_cache[0]

    def scaled(c):
        loads_once("targs")
        err = acc[c] - targs[:, c * COLS : (c + 1) * COLS].astype(F32)
        st[c] = (err.T * factor_row()).astype(BF16)

    def scatter_span(c, name):
        return (0, X_PART[c]) if name == "x" else (X_PART[c], COLS - X_PART[c])

    def share(c, other, k, lo, n):
        cols = pl.ds(pl.multiple_of(blk(other, k) * BLK, BLK), BLK)
        return jnp.dot(st[c, lo : lo + n], feats[:, cols], preferred_element_type=F32)

    def scatter_cross(c, ki):
        k, n = ORDER[ki], X_PART[c]
        xs[c, ki, 0:n] = share(c, 1, k, 0, n).astype(BF16)
        send(("rx", c, k), xs.at[c, ki, pl.ds(0, n)], xr.at[c, ki, pl.ds(0, n)], xdev, 2 + c)

    def crossed(c, k, val):
        ki, n = ORDER.index(k), X_PART[c]
        arrive(("rx", c, k), xr.at[c, ki, pl.ds(0, n)])
        return val + xr[c, ki, 0:n].astype(F32)

    def scatter_first(c, name):
        lo, n = scatter_span(c, name)
        col = 1 if name == "n" else 0
        val = share(c, col, 4, lo, n)
        if name == "x":
            val = crossed(c, 4, val)
        z0[c, col, lo : lo + n] = val.astype(BF16)
        for d in (1, -1):
            hlo, hn = part_of(lo, n, d)
            src, dst = z0.at[c, col, pl.ds(hlo, hn)], zr.at[c, lane(d, 1, col), pl.ds(hlo, hn)]
            send(("r", c, d, 1, name), src, dst, zdev[d], 2 + c)

    def lane(d, s, col):
        return (s - 1) * 4 + col * 2 + (1 - d) // 2

    def scatter_step(c, s, name, d):
        lo, n = scatter_span(c, name)
        col = 1 if name == "n" else 0
        at = lane(d, s, col)
        k = d * (4 - s)
        val = share(c, col, k, lo, n)
        if name == "x":
            val = crossed(c, k, val)
        if s == 1:
            hlo, hn = part_of(lo, n, d)
            olo, on = part_of(lo, n, -d)
            arrive(("r", c, d, s, name), zr.at[c, at, pl.ds(hlo, hn)])
            zr[c, at, olo : olo + on] = val[olo - lo : olo - lo + on].astype(BF16)
            got = zr[c, at, hlo : hlo + hn].astype(F32)
            zr[c, at, hlo : hlo + hn] = (val[hlo - lo : hlo - lo + hn] + got).astype(BF16)
        else:
            arrive(("r", c, d, s, name), zr.at[c, at, pl.ds(lo, n)])
            zr[c, at, lo : lo + n] = (val + zr[c, at, lo : lo + n].astype(F32)).astype(BF16)
        key = ("r", c, d, s + 1, name) if s < 3 else ("r", c, 4, name)
        send(key, zr.at[c, at, pl.ds(lo, n)], zr.at[c, lane(d, s + 1, col), pl.ds(lo, n)], zdev[d], 2 + c)

    def scatter_last(c, name):
        lo, n = scatter_span(c, name)
        col = 1 if name == "n" else 0
        val = share(c, col, 0, lo, n)
        if name == "x":
            val = crossed(c, 0, val)
        arrive(("r", c, 4, name), zr.at[c, pl.ds(lane(1, 4, col), 2), pl.ds(lo, n)])
        for d in (1, -1):
            val = val + zr[c, lane(d, 4, col), lo : lo + n].astype(F32)
        if name == "n":
            fxs[c, 0:n] = val.astype(BF16)
            send(("fin", c), fxs.at[c, pl.ds(0, n)], fxr.at[c, pl.ds(0, n)], xdev, 2 + c)
        else:
            gt[c, lo : lo + n] = val

    def finish(c):
        lo, n = scatter_span(c, "n")
        if n:
            arrive(("fin", c), fxr.at[c, pl.ds(0, n)])
            gt[c, lo : lo + n] += fxr[c, 0:n].astype(F32)
        store(gt.at[c], grad_hbm.at[c])

    stores = []

    def store(src, dst):
        copy = pltpu.make_async_copy(src, dst, store_sem.at[len(stores)])
        copy.start()
        stores.append(copy)

    nb8 = WIDTH // 8 // BLOCK_WIDTH

    def encode():
        loads["exps"].wait()
        loads["pg"].wait()
        signs = sign_table()
        inv = jnp.right_shift(8, exps_ref[...]).astype(F32) * 0.125
        scale = jnp.left_shift(1, exps_ref[...]).astype(F32)
        for p in range(8):
            base = p * nb8
            rows = jnp.concatenate(
                [pg[:, (base + b) * BLOCK_WIDTH : (base + b + 1) * BLOCK_WIDTH] for b in range(nb8)], axis=0
            )
            turned = rotate(rows, signs)
            for b in range(nb8):
                at = slice(b * BLOCK_WIDTH, (b + 1) * BLOCK_WIDTH)
                val = turned[b * 16 : (b + 1) * 16] * inv[:, base + b : base + b + 1]
                enc[p, :, at] = jnp.clip(val, -1.0, 1.0).astype(BF16)
                scl[p, :, at] = jnp.broadcast_to(scale[:, base + b : base + b + 1], (16, BLOCK_WIDTH))
        for k in range(1, 8):
            p = lax.rem(g + k, 8)
            send("enc", enc.at[p], landed.at[k - 1], (xh * 8 + p, f), 4)

    def partial_sum():
        arrive("enc", landed.at[pl.ds(0, 7)])
        total = enc[g].astype(F32)
        for k in range(1, 8):
            total = total + landed[k - 1].astype(F32)
        par_s[...] = total.astype(BF16)
        send("par", par_s, landed.at[7], ((1 - xh) * 8 + g, f), 4)

    def decode():
        arrive("par", landed.at[7])
        val = (par_s[...].astype(F32) + landed[7].astype(F32)) * (1.0 / REPLICAS) * scl[g]
        rows = jnp.concatenate([val[:, b * BLOCK_WIDTH : (b + 1) * BLOCK_WIDTH] for b in range(nb8)], axis=0)
        turned = rotate(rows, sign_table()).astype(BF16)
        mine = pl.ds(pl.multiple_of(g * 1024, 1024), 1024)
        dlt[:, mine] = jnp.concatenate([turned[b * 16 : (b + 1) * 16] for b in range(nb8)], axis=1)
        for k in range(1, 8):
            send("dlt", dlt.at[:, mine], dlt.at[:, mine], (xh * 8 + lax.rem(g + k, 8), f), 4)

    def update():
        arrive("dlt", landed.at[pl.ds(0, 7)])
        store(dlt, delta_hbm)

    steps = {
        "gs": gather_start,
        "gc": gather_cross,
        "gf": gather_forward,
        "gp": product,
        "sc": scaled,
        "rc": scatter_cross,
        "rf": scatter_first,
        "rs": scatter_step,
        "rl": scatter_last,
        "fin": finish,
        "enc": encode,
        "par": partial_sum,
        "dec": decode,
        "upd": update,
    }
    for step in PLAN:
        steps[step[0]](*step[1:])
    assert len(slots) == N_SLOTS, len(slots)

    for c in range(CHUNKS):
        sent(c, wg.at[c, pl.ds(0, 15), pl.ds(0, BLK if c else BLK + EXTRA)])
        sent(2 + c, zr.at[c, pl.ds(0, 15)])
    sent(4, landed)
    for copy in stores:
        copy.wait()


def finish_kernel(gt_hbm, delta_hbm, params_hbm, moment_hbm, grad_hbm, newp_hbm, newm_hbm, gt, dlt, params, moment, out, newp, newm, load_sem, store_sem):
    loads = [
        pltpu.make_async_copy(gt_hbm.at[c], gt.at[c], load_sem.at[c]) for c in range(CHUNKS)
    ] + [
        pltpu.make_async_copy(delta_hbm, dlt, load_sem.at[CHUNKS]),
        pltpu.make_async_copy(params_hbm, params, load_sem.at[CHUNKS + 1]),
        pltpu.make_async_copy(moment_hbm, moment, load_sem.at[CHUNKS + 2]),
    ]
    for copy in loads:
        copy.start()
    stores = []

    def store(src, dst):
        copy = pltpu.make_async_copy(src, dst, store_sem.at[len(stores)])
        copy.start()
        stores.append(copy)

    for c in range(CHUNKS):
        loads[c].wait()
        out[:, c * COLS : (c + 1) * COLS] = gt[c].T
    store(out, grad_hbm.at[0])
    for copy in loads[CHUNKS:]:
        copy.wait()
    delta = dlt[...].astype(F32)
    new = MOMENTUM * moment[...] + delta
    newm[...] = new
    store(newm, newm_hbm)
    newp[...] = params[...] - OUTER_RATE * (delta + MOMENTUM * new)
    store(newp, newp_hbm)
    for copy in stores:
        copy.wait()


def on_device(features, targets, value_weight, segment_ids, traj_counts, pseudo_grad, block_exps, outer_params, outer_moment):
    hbm = pl.BlockSpec(memory_space=pl.ANY)
    xmax = max(X_PART)
    zmax = COLS - min(X_PART)
    out = pl.pallas_call(
        kernel,
        out_shape=(
            jax.ShapeDtypeStruct((CHUNKS, COLS, BLK), F32),
            jax.ShapeDtypeStruct((16, WIDTH), BF16),
        ),
        in_specs=[hbm] * 7,
        out_specs=(hbm, hbm),
        scratch_shapes=[
            pltpu.VMEM((TOK, WIDTH), BF16),
            pltpu.VMEM((TOK, 2 * COLS), BF16),
            pltpu.VMEM((CHUNKS, 16, BLK + EXTRA, COLS), BF16),
            pltpu.VMEM((CHUNKS, TOK, COLS), F32),
            pltpu.VMEM((CHUNKS, COLS, TOK), BF16),
            pltpu.VMEM((CHUNKS, 8, xmax, BLK), BF16),
            pltpu.VMEM((CHUNKS, 8, xmax, BLK), BF16),
            pltpu.VMEM((CHUNKS, 2, COLS, BLK), BF16),
            pltpu.VMEM((CHUNKS, 16, COLS, BLK), BF16),
            pltpu.VMEM((CHUNKS, zmax, BLK), BF16),
            pltpu.VMEM((CHUNKS, zmax, BLK), BF16),
            pltpu.VMEM((CHUNKS, COLS, BLK), F32),
            pltpu.VMEM((CHUNKS, BLK, COLS), F32),
            pltpu.VMEM((16, WIDTH), F32),
            pltpu.VMEM((8, 16, 1024), F32),
            pltpu.VMEM((8, 16, 1024), BF16),
            pltpu.VMEM((15, 16, 1024), BF16),
            pltpu.VMEM((16, 1024), BF16),
            pltpu.VMEM((16, WIDTH), BF16),
            pltpu.VMEM((1, TOK), jnp.int32),
            pltpu.VMEM((1, 8), jnp.int32),
            pltpu.VMEM((16, WIDTH // BLOCK_WIDTH), jnp.int32),
            pltpu.SemaphoreType.DMA((CHUNKS + 6,)),
            pltpu.SemaphoreType.DMA((3,)),
            pltpu.SemaphoreType.DMA((5,)),
            pltpu.SemaphoreType.DMA((N_SLOTS,)),
        ],
        compiler_params=pltpu.CompilerParams(
            collective_id=0, has_side_effects=True, vmem_limit_bytes=56 * 2**20
        ),
    )(features, targets, value_weight, segment_ids, traj_counts, pseudo_grad, block_exps)
    wide = pltpu.VMEM((16, WIDTH), F32)
    return pl.pallas_call(
        finish_kernel,
        out_shape=(
            jax.ShapeDtypeStruct((1, BLK, CHUNKS * COLS), F32),
            jax.ShapeDtypeStruct((16, WIDTH), F32),
            jax.ShapeDtypeStruct((16, WIDTH), F32),
        ),
        in_specs=[hbm] * 4,
        out_specs=(hbm,) * 3,
        scratch_shapes=[
            pltpu.VMEM((CHUNKS, COLS, BLK), F32),
            pltpu.VMEM((16, WIDTH), BF16),
            wide,
            wide,
            pltpu.VMEM((BLK, CHUNKS * COLS), F32),
            wide,
            wide,
            pltpu.SemaphoreType.DMA((CHUNKS + 3,)),
            pltpu.SemaphoreType.DMA((3,)),
        ],
        compiler_params=pltpu.CompilerParams(vmem_limit_bytes=60 * 2**20),
    )(*out, outer_params, outer_moment)


def solution(mesh):
    return jax.shard_map(
        on_device,
        mesh=mesh,
        in_specs=(
            P("rep", "fsdp", None),
            P("rep", "fsdp", None),
            P("rep", "fsdp", None),
            P("rep", "fsdp"),
            P("rep", "fsdp"),
            P("rep", "fsdp", None),
            P("fsdp", None),
            P("fsdp", None),
            P("fsdp", None),
        ),
        out_specs=(P("rep", "fsdp", None), P("fsdp", None), P("fsdp", None)),
        check_vma=False,
    )
```

time: 408 us -> 134 us (0.33)
  waiting for transfers between devices: 320 us -> 0 us
  Pallas kernels: 0 us -> 133 us
  blocking collectives: 37.6 us -> 0 us
  matrix products: 24.8 us -> 0 us
  between operations: 15.5 us -> 0.8 us
  other arithmetic: 5.44 us -> 0 us
    psum x1 -> x0, waiting for transfers between devices: 258 us -> none  [on_device(): lax.psum(encoded_wide.astype(jnp.bfloat16), 'rep').astype(jnp.float32)]
    pallas_call x0 -> x2, Pallas kernels: none -> 133 us  [the longest x1 130 us: on_device(): pl.pallas_call(kernel, out_shape=(jax.ShapeDtypeStruct((CHUNKS, COLS, BLK...]
    all_gather x1 -> x0, waiting for transfers between devices: 61.3 us -> none  [on_device(): lax.all_gather(value_weight[0], 'fsdp', axis=0, tiled=True)]
    psum x1 -> x0, blocking collectives: 37.6 us -> none  [on_device(): live_total = lax.psum(jnp.sum(live.astype(jnp.float32)), 'fsdp')]
    dot_general x4 -> x0, matrix products: 24.8 us -> none  [the longest x1 11.6 us: on_device(): lax.dot_general(columns, scaled, (((0,), (0,)), ((), ())), preferred_elem...]
  transfers between devices with their start and end apart: 3 -> 0, of which waited for: 2 -> 0; matrix products, arithmetic and copies ran while one was open for 8% -> 0% of each run, Pallas kernels for 0% -> 0%
where the time goes in v2:
time: 134 us
  Pallas kernels  133 us (99%)
    pallas_call x1, Pallas kernels, on_device(): pl.pallas_call(kernel, out_shape=(jax.ShapeDtypeStruct((CHUNKS, COLS, BLK...  130 us
    pallas_call x1, Pallas kernels, on_device(): pl.pallas_call(finish_kernel, out_shape=(jax.ShapeDtypeStruct((1, BLK, CH...  2.83 us

profile of v2, /device:TPU:2, one launch (start us, length us, event | category | flops | bytes accessed | tf_op | source)
XLA Modules:
  0.0 133.7 jit_solution(14381097309084178726)
XLA Ops:
  0.6 130.0 %shard_map.112 = (f32[2,256,512]{2,1,0:T(8,128)}, bf16[16,8192]{1,0:T(8,128)(2,1)}) custom-call(bf16[1,512,8192]{2,1,0:T(8,128)(2,1)} %feats_hbm.1, bf16[1,512,512]{2,1,0:T(8,128)(2,1)} %targs_hbm.1, bf16[1,512,512]{2,1,0:T(8,128)(2,1)} %weight_hbm.1, s32[1,512]{1,0:T(1,128)} %seg_hbm.1, s32[1,8]{1,0:T(1,128)} %counts_hbm.1, f32[1,16,8192]{2,1,0:T(8,128)} %pg_hbm.1, ...), custom_call_target="tpu_custom_call" | custom-call | tf_op jit(solution)/shard_map/pallas_call | solution.py:436
  130.7 2.8 %shard_map.113 = (f32[1,512,512]{2,1,0:T(8,128)}, f32[16,8192]{1,0:T(8,128)}, f32[16,8192]{1,0:T(8,128)}) custom-call(f32[2,256,512]{2,1,0:T(8,128)} %get-tuple-element.5.gt_hbm, bf16[16,8192]{1,0:T(8,128)(2,1)} %get-tuple-element.6.delta_hbm, f32[16,8192]{1,0:T(8,128)} %params_hbm.1, f32[16,8192]{1,0:T(8,128)} %moment_hbm.1), custom_call_target="tpu_custom_call" | custom-call | tf_op jit(solution)/shard_map/pallas_call | solution.py:477

commit v3 on v2

--- a/solution.py
+++ b/solution.py
@@ -19,48 +19,55 @@
 TOK = 512
 WIDTH = 8192
 COLS = 256
+HALF = 256
 CHUNKS = 2
-N_SLOTS = 123
+N_SLOTS = 124
 EXTRA = 32
-X_ROWS = (320, 192)
-X_PART = (160, 160)
+X_ROWS = (HALF, HALF)
+X_PART = (64, 256)
 ORDER = (4, 3, -3, 2, -2, 1, -1, 0)
+COLUMN = {"o": 0, "x": 0, "n": 1, "b": 2}
 F32 = jnp.float32
 BF16 = jnp.bfloat16
 PLAN = (
-    ("gs", 0), ("gc", 0), ("gf", 0, 1, "o", 1), ("gf", 0, 1, "o", -1),
-    ("enc",), ("gp", 0, 0), ("gf", 0, 1, "x", 1), ("gf", 0, 1, "x", -1),
-    ("gf", 0, 1, "n", 1), ("gf", 0, 1, "n", -1), ("par",), ("gf", 0, 2, "o", 1),
-    ("gf", 0, 2, "o", -1), ("gf", 0, 2, "x", 1), ("gf", 0, 2, "x", -1), ("gp", 0, 1),
-    ("gf", 0, 2, "n", 1), ("gf", 0, 2, "n", -1), ("dec",), ("gf", 0, 3, "o", 1),
-    ("gf", 0, 3, "o", -1), ("gf", 0, 3, "x", 1), ("gf", 0, 3, "x", -1), ("upd",),
-    ("gp", 0, 2), ("gf", 0, 3, "n", 1), ("gf", 0, 3, "n", -1), ("gs", 1),
-    ("gf", 0, 4, "o", 1), ("gf", 0, 4, "o", -1), ("gf", 0, 4, "x", 1), ("gf", 0, 4, "x", -1),
-    ("gf", 0, 4, "n", 1), ("gf", 0, 4, "n", -1), ("gp", 0, 3), ("gf", 1, 1, "o", 1),
-    ("gf", 1, 1, "o", -1), ("gf", 1, 1, "x", 1), ("gf", 1, 1, "x", -1), ("gc", 1),
-    ("gp", 1, 0), ("gf", 1, 2, "o", 1), ("gf", 1, 2, "o", -1), ("gf", 1, 2, "x", 1),
-    ("gf", 1, 2, "x", -1), ("gp", 0, 4), ("sc", 0), ("gf", 1, 1, "n", 1),
-    ("gf", 1, 1, "n", -1), ("gp", 1, 1), ("rc", 0, 0), ("gf", 1, 3, "o", 1),
-    ("gf", 1, 3, "o", -1), ("gf", 1, 3, "x", 1), ("gf", 1, 3, "x", -1), ("rf", 0, "o"),
-    ("gf", 1, 2, "n", 1), ("gf", 1, 2, "n", -1), ("gp", 1, 2), ("rc", 0, 1),
-    ("gf", 1, 4, "o", 1), ("gf", 1, 4, "o", -1), ("gf", 1, 4, "x", 1), ("gf", 1, 4, "x", -1),
-    ("rs", 0, 1, "o", 1), ("rs", 0, 1, "o", -1), ("rf", 0, "n"), ("rc", 0, 2),
-    ("gf", 1, 3, "n", 1), ("gf", 1, 3, "n", -1), ("gp", 1, 3), ("rf", 0, "x"),
-    ("rs", 0, 2, "o", 1), ("rs", 0, 2, "o", -1), ("rc", 0, 3), ("rs", 0, 1, "n", 1),
-    ("rs", 0, 1, "n", -1), ("gf", 1, 4, "n", 1), ("gf", 1, 4, "n", -1), ("gp", 1, 4),
-    ("sc", 1), ("rc", 0, 4), ("rs", 0, 1, "x", 1), ("rs", 0, 1, "x", -1),
-    ("rs", 0, 3, "o", 1), ("rs", 0, 3, "o", -1), ("rc", 0, 5), ("rs", 0, 2, "n", 1),
-    ("rs", 0, 2, "n", -1), ("rc", 0, 6), ("rs", 0, 2, "x", 1), ("rs", 0, 2, "x", -1),
-    ("rl", 0, "o"), ("rc", 0, 7), ("rs", 0, 3, "n", 1), ("rs", 0, 3, "n", -1),
-    ("rc", 1, 0), ("rf", 1, "o"), ("rs", 0, 3, "x", 1), ("rs", 0, 3, "x", -1),
-    ("rc", 1, 1), ("rl", 0, "n"), ("rs", 1, 1, "o", 1), ("rs", 1, 1, "o", -1),
-    ("rf", 1, "n"), ("rf", 1, "x"), ("rl", 0, "x"), ("rc", 1, 2),
-    ("rs", 1, 2, "o", 1), ("rs", 1, 2, "o", -1), ("rs", 1, 1, "n", 1), ("rs", 1, 1, "n", -1),
-    ("fin", 0), ("rc", 1, 3), ("rs", 1, 1, "x", 1), ("rs", 1, 3, "o", 1),
-    ("rs", 1, 3, "o", -1), ("rs", 1, 1, "x", -1), ("rc", 1, 4), ("rs", 1, 2, "n", 1),
-    ("rs", 1, 2, "n", -1), ("rc", 1, 5), ("rs", 1, 2, "x", 1), ("rl", 1, "o"),
-    ("rc", 1, 6), ("rs", 1, 2, "x", -1), ("rs", 1, 3, "n", 1), ("rs", 1, 3, "n", -1),
-    ("rc", 1, 7), ("rs", 1, 3, "x", 1), ("rs", 1, 3, "x", -1), ("rl", 1, "n"),
+    ("gs", 0), ("fx", 0), ("gc", 0), ("gp", 0, 0),
+    ("gf", 0, 1, "o", 1), ("gf", 0, 1, "o", -1), ("enc",), ("fx", 1),
+    ("gf", 0, 1, "x", 1), ("gf", 0, 1, "x", -1), ("gf", 0, 1, "n", 1), ("gf", 0, 1, "n", -1),
+    ("gp", 0, 1), ("fx", 2), ("par",), ("gf", 0, 2, "o", 1),
+    ("gf", 0, 2, "o", -1), ("gf", 0, 2, "x", 1), ("gf", 0, 2, "x", -1), ("fx", 3),
+    ("dec",), ("gf", 0, 2, "n", 1), ("gf", 0, 2, "n", -1), ("gp", 0, 2),
+    ("gf", 0, 3, "o", 1), ("gf", 0, 3, "o", -1), ("fx", 4), ("upd",),
+    ("gf", 0, 3, "x", 1), ("gf", 0, 3, "x", -1), ("fx", 5), ("gf", 0, 3, "n", 1),
+    ("gf", 0, 3, "n", -1), ("gp", 0, 3), ("gs", 1), ("gf", 0, 4, "o", 1),
+    ("gf", 0, 4, "o", -1), ("gf", 0, 4, "x", 1), ("gf", 0, 4, "x", -1), ("gf", 0, 4, "n", 1),
+    ("gf", 0, 4, "n", -1), ("gp", 0, 4), ("gf", 1, 1, "o", 1), ("gf", 1, 1, "o", -1),
+    ("fx", 6), ("gf", 1, 1, "x", 1), ("gf", 1, 1, "x", -1), ("gf", 1, 2, "o", 1),
+    ("gf", 1, 2, "o", -1), ("gc", 1), ("gp", 1, 0), ("fx", 7),
+    ("gf", 1, 2, "x", 1), ("gf", 1, 2, "x", -1), ("gf", 1, 3, "o", 1), ("gf", 1, 3, "o", -1),
+    ("gf", 1, 1, "n", 1), ("gf", 1, 1, "n", -1), ("gp", 1, 1), ("gq", 0, 0),
+    ("gq", 0, 1), ("gf", 1, 3, "x", 1), ("gf", 1, 3, "x", -1), ("gq", 0, 2),
+    ("gq", 0, 3), ("gq", 0, 4), ("gq", 1, 0), ("gq", 1, 1),
+    ("gf", 1, 4, "o", 1), ("gf", 1, 4, "o", -1), ("gf", 1, 2, "n", 1), ("gf", 1, 2, "n", -1),
+    ("gp", 1, 2), ("gq", 1, 2), ("gf", 1, 4, "x", 1), ("gf", 1, 4, "x", -1),
+    ("sc", 0), ("ss", 0), ("rf", 0, "o"), ("rf", 0, "n"),
+    ("gf", 1, 3, "n", 1), ("gf", 1, 3, "n", -1), ("gp", 1, 3), ("gq", 1, 3),
+    ("rc", 0, 0), ("rc", 0, 1), ("rs", 0, 1, "o", 1), ("rs", 0, 1, "o", -1),
+    ("rc", 0, 2), ("rs", 0, 1, "n", 1), ("rs", 0, 1, "n", -1), ("rc", 0, 3),
+    ("rc", 0, 4), ("gf", 1, 4, "n", 1), ("rc", 0, 5), ("gf", 1, 4, "n", -1),
+    ("gp", 1, 4), ("gq", 1, 4), ("rf", 0, "b"), ("rs", 0, 2, "o", 1),
+    ("rs", 0, 2, "o", -1), ("rf", 0, "x"), ("rs", 0, 2, "n", 1), ("rs", 0, 2, "n", -1),
+    ("rs", 0, 1, "b", 1), ("rs", 0, 1, "b", -1), ("rc", 0, 6), ("rc", 0, 7),
+    ("rs", 0, 3, "o", 1), ("rs", 0, 3, "o", -1), ("rs", 0, 1, "x", 1), ("rs", 0, 1, "x", -1),
+    ("rs", 0, 3, "n", 1), ("rs", 0, 3, "n", -1), ("sc", 1), ("ss", 1),
+    ("rs", 0, 2, "b", 1), ("rs", 0, 2, "b", -1), ("rc", 1, 0), ("rl", 0, "o"),
+    ("rs", 0, 2, "x", 1), ("rs", 0, 2, "x", -1), ("rc", 1, 1), ("rl", 0, "n"),
+    ("rf", 1, "b"), ("rs", 0, 3, "b", 1), ("rs", 0, 3, "b", -1), ("rc", 1, 2),
+    ("rs", 0, 3, "x", 1), ("rs", 0, 3, "x", -1), ("rf", 1, "x"), ("rs", 1, 1, "b", 1),
+    ("rs", 1, 1, "b", -1), ("rc", 1, 3), ("rl", 0, "b"), ("rc", 1, 4),
+    ("rl", 0, "x"), ("fin", 0), ("rs", 1, 1, "x", 1), ("rs", 1, 1, "x", -1),
+    ("rc", 1, 5), ("rs", 1, 2, "b", 1), ("rs", 1, 2, "b", -1), ("rc", 1, 6),
+    ("rs", 1, 2, "x", 1), ("rs", 1, 2, "x", -1), ("rc", 1, 7), ("rs", 1, 3, "b", 1),
+    ("rs", 1, 3, "b", -1), ("rs", 1, 3, "x", 1), ("rs", 1, 3, "x", -1), ("rl", 1, "b"),
     ("rl", 1, "x"), ("fin", 1),
 )
 
@@ -88,7 +95,7 @@
 def kernel(
     feats_hbm, targs_hbm, weight_hbm, seg_hbm, counts_hbm, pg_hbm, exps_hbm,
     grad_hbm, delta_hbm,
-    feats, targs, wg, acc, st, xs, xr, z0, zr, fxs, fxr, gt, outw,
+    feats, targs, wg, acc, st, fnb, accn, ps, pr, stn, xs, xr, z0, zr, fxs, fxr, gt, outw,
     pg, scl, enc, landed, par_s, dlt,
     seg_ref, counts_ref, exps_ref, load_sem, store_sem, ss, rs,
 ):
@@ -159,7 +166,7 @@
 
     def gather_push(key, c, j, lo, n, target):
         ref = wg.at[c, j, pl.ds(lo, n)]
-        send(key, ref, ref, target, c)
+        send(key, ref, ref, target, 2 + c if lo < HALF else c)
 
     def gather_span(c, name):
         return (0, X_ROWS[c]) if name == "x" else (X_ROWS[c], BLK - X_ROWS[c] + (0 if c else EXTRA))
@@ -178,8 +185,6 @@
             if n:
                 for d in (1, -1):
                     gather_push(("g", c, d, 1, name), c, own, lo, n, zdev[d])
-        if n:
-            gather_push(("gx", c, 0), c, own, lo, n, xdev)
 
     def gather_cross(c):
         lo, n = gather_span(c, "n")
@@ -195,28 +200,40 @@
         if s < 4:
             at = (lo, n) if s < 3 else half
             gather_push(("g", c, d, s + 1, name), c, j, *at, zdev[d])
-        if name == "x":
-            at = (lo, n) if s < 4 else half
-            gather_push(("gx", c, s), c, j, *at, xdev)
 
     def product(c, k):
         if k == 0:
             loads_once("feats")
-        if X_ROWS[c]:
-            lo, n = gather_span(c, "x")
-            if k in (0, 4):
-                arrive(("gx", c, k), wg.at[c, blk(1, k), pl.ds(lo, n)])
-            else:
-                arrive(("gx", c, k), wg.at[c, pl.ds(0, 2), pl.ds(lo, n)])
         for kk in (k,) if k in (0, 4) else (k, -k):
             for other in (0, 1):
                 j = blk(other, kk)
-                cols = pl.ds(pl.multiple_of(j * BLK, BLK), BLK)
-                part = jnp.dot(feats[:, cols], wg[c, j, 0:BLK], preferred_element_type=F32)
+                lo = HALF if other else 0
+                cols = pl.ds(pl.multiple_of(j * BLK + lo, HALF), BLK - lo)
+                part = jnp.dot(feats[:, cols], wg[c, j, lo:BLK], preferred_element_type=F32)
                 if (kk, other) == (0, 0):
                     acc[c] = part
                 else:
                     acc[c] += part
+
+    def lend(ki):
+        loads_once("feats")
+        cols = pl.ds(pl.multiple_of(blk(1, ORDER[ki]) * BLK, BLK), HALF)
+        send(("fx", ki), feats.at[:, cols], fnb.at[ki], xdev, 9)
+
+    def product_lent(c, k):
+        for kk in (k,) if k in (0, 4) else (k, -k):
+            ki = ORDER.index(kk)
+            if ki not in waited:
+                waited.add(ki)
+                arrive(("fx", ki), fnb.at[ki])
+            part = jnp.dot(fnb[ki], wg[c, blk(0, kk), 0:HALF], preferred_element_type=F32)
+            if kk == 0:
+                accn[c] = part
+            else:
+                accn[c] += part
+        if k == 4:
+            ps[c] = accn[c].astype(BF16)
+            send(("pn", c), ps.at[c], pr.at[c], xdev, 9)
 
     waited = set()
 
@@ -238,20 +255,31 @@
 
     def scaled(c):
         loads_once("targs")
-        err = acc[c] - targs[:, c * COLS : (c + 1) * COLS].astype(F32)
+        arrive(("pn", c), pr.at[c])
+        err = acc[c] + pr[c].astype(F32) - targs[:, c * COLS : (c + 1) * COLS].astype(F32)
         st[c] = (err.T * factor_row()).astype(BF16)
 
+    def lend_scaled(c):
+        send(("sn", c), st.at[c], stn.at[c], xdev, 9)
+
     def scatter_span(c, name):
+        if name == "b":
+            return 0, COLS
         return (0, X_PART[c]) if name == "x" else (X_PART[c], COLS - X_PART[c])
 
-    def share(c, other, k, lo, n):
-        cols = pl.ds(pl.multiple_of(blk(other, k) * BLK, BLK), BLK)
-        return jnp.dot(st[c, lo : lo + n], feats[:, cols], preferred_element_type=F32)
+    def share(c, name, k):
+        lo, n = scatter_span(c, "x" if name == "c" else name)
+        start = blk(name in ("n", "c"), k) * BLK + (0 if name == "b" else HALF)
+        cols = pl.ds(pl.multiple_of(start, HALF), HALF)
+        val = jnp.dot(st[c, lo : lo + n], feats[:, cols], preferred_element_type=F32)
+        if name == "b":
+            val = val + jnp.dot(stn[c], fnb[ORDER.index(k)], preferred_element_type=F32)
+        return val
 
     def scatter_cross(c, ki):
         k, n = ORDER[ki], X_PART[c]
-        xs[c, ki, 0:n] = share(c, 1, k, 0, n).astype(BF16)
-        send(("rx", c, k), xs.at[c, ki, pl.ds(0, n)], xr.at[c, ki, pl.ds(0, n)], xdev, 2 + c)
+        xs[c, ki, 0:n] = share(c, "c", k).astype(BF16)
+        send(("rx", c, k), xs.at[c, ki, pl.ds(0, n)], xr.at[c, ki, pl.ds(0, n)], xdev, 4 + c)
 
     def crossed(c, k, val):
         ki, n = ORDER.index(k), X_PART[c]
@@ -260,25 +288,28 @@
 
     def scatter_first(c, name):
         lo, n = scatter_span(c, name)
-        col = 1 if name == "n" else 0
-        val = share(c, col, 4, lo, n)
+        col = COLUMN[name]
+        if name == "b":
+            arrive(("sn", c), stn.at[c])
+        val = share(c, name, 4)
         if name == "x":
             val = crossed(c, 4, val)
         z0[c, col, lo : lo + n] = val.astype(BF16)
+        group = 6 + c if name == "b" else 4 + c
         for d in (1, -1):
             hlo, hn = part_of(lo, n, d)
             src, dst = z0.at[c, col, pl.ds(hlo, hn)], zr.at[c, lane(d, 1, col), pl.ds(hlo, hn)]
-            send(("r", c, d, 1, name), src, dst, zdev[d], 2 + c)
+            send(("r", c, d, 1, name), src, dst, zdev[d], group)
 
     def lane(d, s, col):
-        return (s - 1) * 4 + col * 2 + (1 - d) // 2
+        return (16 + (s - 1) * 2 if col == 2 else (s - 1) * 4 + col * 2) + (1 - d) // 2
 
     def scatter_step(c, s, name, d):
         lo, n = scatter_span(c, name)
-        col = 1 if name == "n" else 0
+        col = COLUMN[name]
         at = lane(d, s, col)
         k = d * (4 - s)
-        val = share(c, col, k, lo, n)
+        val = share(c, name, k)
         if name == "x":
             val = crossed(c, k, val)
         if s == 1:
@@ -292,12 +323,12 @@
             arrive(("r", c, d, s, name), zr.at[c, at, pl.ds(lo, n)])
             zr[c, at, lo : lo + n] = (val + zr[c, at, lo : lo + n].astype(F32)).astype(BF16)
         key = ("r", c, d, s + 1, name) if s < 3 else ("r", c, 4, name)
-        send(key, zr.at[c, at, pl.ds(lo, n)], zr.at[c, lane(d, s + 1, col), pl.ds(lo, n)], zdev[d], 2 + c)
+        send(key, zr.at[c, at, pl.ds(lo, n)], zr.at[c, lane(d, s + 1, col), pl.ds(lo, n)], zdev[d], (6 if col == 2 else 4) + c)
 
     def scatter_last(c, name):
         lo, n = scatter_span(c, name)
-        col = 1 if name == "n" else 0
-        val = share(c, col, 0, lo, n)
+        col = COLUMN[name]
+        val = share(c, name, 0)
         if name == "x":
             val = crossed(c, 0, val)
         arrive(("r", c, 4, name), zr.at[c, pl.ds(lane(1, 4, col), 2), pl.ds(lo, n)])
@@ -305,15 +336,17 @@
             val = val + zr[c, lane(d, 4, col), lo : lo + n].astype(F32)
         if name == "n":
             fxs[c, 0:n] = val.astype(BF16)
-            send(("fin", c), fxs.at[c, pl.ds(0, n)], fxr.at[c, pl.ds(0, n)], xdev, 2 + c)
+            send(("fin", c), fxs.at[c, pl.ds(0, n)], fxr.at[c, pl.ds(0, n)], xdev, 4 + c)
+        elif name == "b":
+            gt[c, :, 0:HALF] = val
         else:
-            gt[c, lo : lo + n] = val
+            gt[c, lo : lo + n, HALF:] = val
 
     def finish(c):
         lo, n = scatter_span(c, "n")
         if n:
             arrive(("fin", c), fxr.at[c, pl.ds(0, n)])
-            gt[c, lo : lo + n] += fxr[c, 0:n].astype(F32)
+            gt[c, lo : lo + n, HALF:] += fxr[c, 0:n].astype(F32)
         store(gt.at[c], grad_hbm.at[c])
 
     stores = []
@@ -344,7 +377,7 @@
                 scl[p, :, at] = jnp.broadcast_to(scale[:, base + b : base + b + 1], (16, BLOCK_WIDTH))
         for k in range(1, 8):
             p = lax.rem(g + k, 8)
-            send("enc", enc.at[p], landed.at[k - 1], (xh * 8 + p, f), 4)
+            send("enc", enc.at[p], landed.at[k - 1], (xh * 8 + p, f), 8)
 
     def partial_sum():
         arrive("enc", landed.at[pl.ds(0, 7)])
@@ -352,7 +385,7 @@
         for k in range(1, 8):
             total = total + landed[k - 1].astype(F32)
         par_s[...] = total.astype(BF16)
-        send("par", par_s, landed.at[7], ((1 - xh) * 8 + g, f), 4)
+        send("par", par_s, landed.at[7], ((1 - xh) * 8 + g, f), 8)
 
     def decode():
         arrive("par", landed.at[7])
@@ -362,7 +395,7 @@
         mine = pl.ds(pl.multiple_of(g * 1024, 1024), 1024)
         dlt[:, mine] = jnp.concatenate([turned[b * 16 : (b + 1) * 16] for b in range(nb8)], axis=1)
         for k in range(1, 8):
-            send("dlt", dlt.at[:, mine], dlt.at[:, mine], (xh * 8 + lax.rem(g + k, 8), f), 4)
+            send("dlt", dlt.at[:, mine], dlt.at[:, mine], (xh * 8 + lax.rem(g + k, 8), f), 8)
 
     def update():
         arrive("dlt", landed.at[pl.ds(0, 7)])
@@ -373,6 +406,9 @@
         "gc": gather_cross,
         "gf": gather_forward,
         "gp": product,
+        "fx": lend,
+        "gq": product_lent,
+        "ss": lend_scaled,
         "sc": scaled,
         "rc": scatter_cross,
         "rf": scatter_first,
@@ -389,9 +425,13 @@
     assert len(slots) == N_SLOTS, len(slots)
 
     for c in range(CHUNKS):
-        sent(c, wg.at[c, pl.ds(0, 15), pl.ds(0, BLK if c else BLK + EXTRA)])
-        sent(2 + c, zr.at[c, pl.ds(0, 15)])
-    sent(4, landed)
+        lo, n = gather_span(c, "o")
+        sent(c, wg.at[c, pl.ds(0, 15), pl.ds(lo, n)])
+        sent(2 + c, wg.at[c, pl.ds(0, 7), pl.ds(0, HALF)])
+        sent(4 + c, zr.at[c, pl.ds(0, 15)])
+        sent(6 + c, zr.at[c, pl.ds(0, 7)])
+    sent(8, landed)
+    sent(9, zr.at[0, pl.ds(0, 24)])
     for copy in stores:
         copy.wait()
 
@@ -447,12 +487,17 @@
             pltpu.VMEM((CHUNKS, 16, BLK + EXTRA, COLS), BF16),
             pltpu.VMEM((CHUNKS, TOK, COLS), F32),
             pltpu.VMEM((CHUNKS, COLS, TOK), BF16),
-            pltpu.VMEM((CHUNKS, 8, xmax, BLK), BF16),
-            pltpu.VMEM((CHUNKS, 8, xmax, BLK), BF16),
-            pltpu.VMEM((CHUNKS, 2, COLS, BLK), BF16),
-            pltpu.VMEM((CHUNKS, 16, COLS, BLK), BF16),
-            pltpu.VMEM((CHUNKS, zmax, BLK), BF16),
-            pltpu.VMEM((CHUNKS, zmax, BLK), BF16),
+            pltpu.VMEM((8, TOK, HALF), BF16),
+            pltpu.VMEM((CHUNKS, TOK, COLS), F32),
+            pltpu.VMEM((CHUNKS, TOK, COLS), BF16),
+            pltpu.VMEM((CHUNKS, TOK, COLS), BF16),
+            pltpu.VMEM((CHUNKS, COLS, TOK), BF16),
+            pltpu.VMEM((CHUNKS, 8, xmax, HALF), BF16),
+            pltpu.VMEM((CHUNKS, 8, xmax, HALF), BF16),
+            pltpu.VMEM((CHUNKS, 3, COLS, HALF), BF16),
+            pltpu.VMEM((CHUNKS, 24, COLS, HALF), BF16),
+            pltpu.VMEM((CHUNKS, zmax, HALF), BF16),
+            pltpu.VMEM((CHUNKS, zmax, HALF), BF16),
             pltpu.VMEM((CHUNKS, COLS, BLK), F32),
             pltpu.VMEM((CHUNKS, BLK, COLS), F32),
             pltpu.VMEM((16, WIDTH), F32),
@@ -466,7 +511,7 @@
             pltpu.VMEM((16, WIDTH // BLOCK_WIDTH), jnp.int32),
             pltpu.SemaphoreType.DMA((CHUNKS + 6,)),
             pltpu.SemaphoreType.DMA((3,)),
-            pltpu.SemaphoreType.DMA((5,)),
+            pltpu.SemaphoreType.DMA((10,)),
             pltpu.SemaphoreType.DMA((N_SLOTS,)),
         ],
         compiler_params=pltpu.CompilerParams(

time: 134 us -> 127 us (0.948)
  Pallas kernels: 133 us -> 126 us
    pallas_call x1, Pallas kernels: 130 us -> 124 us  [on_device(): pl.pallas_call(kernel, out_shape=(jax.ShapeDtypeStruct((CHUNKS, COLS, BLK...]
where the time goes in v3:
time: 127 us
  Pallas kernels  126 us (99%)
    pallas_call x1, Pallas kernels, on_device(): pl.pallas_call(kernel, out_shape=(jax.ShapeDtypeStruct((CHUNKS, COLS, BLK...  124 us
    pallas_call x1, Pallas kernels, on_device(): pl.pallas_call(finish_kernel, out_shape=(jax.ShapeDtypeStruct((1, BLK, CH...  2.83 us

profile of v3, /device:TPU:2, one launch (start us, length us, event | category | flops | bytes accessed | tf_op | source)
XLA Modules:
  0.0 127.3 jit_solution(4164958707414885849)
XLA Ops:
  0.6 123.6 %shard_map.112 = (f32[2,256,512]{2,1,0:T(8,128)}, bf16[16,8192]{1,0:T(8,128)(2,1)}) custom-call(bf16[1,512,8192]{2,1,0:T(8,128)(2,1)} %feats_hbm.1, bf16[1,512,512]{2,1,0:T(8,128)(2,1)} %targs_hbm.1, bf16[1,512,512]{2,1,0:T(8,128)(2,1)} %weight_hbm.1, s32[1,512]{1,0:T(1,128)} %seg_hbm.1, s32[1,8]{1,0:T(1,128)} %counts_hbm.1, f32[1,16,8192]{2,1,0:T(8,128)} %pg_hbm.1, ...), custom_call_target="tpu_custom_call" | custom-call | tf_op jit(solution)/shard_map/pallas_call | solution.py:476
  124.3 2.8 %shard_map.113 = (f32[1,512,512]{2,1,0:T(8,128)}, f32[16,8192]{1,0:T(8,128)}, f32[16,8192]{1,0:T(8,128)}) custom-call(f32[2,256,512]{2,1,0:T(8,128)} %get-tuple-element.5.gt_hbm, bf16[16,8192]{1,0:T(8,128)(2,1)} %get-tuple-element.6.delta_hbm, f32[16,8192]{1,0:T(8,128)} %params_hbm.1, f32[16,8192]{1,0:T(8,128)} %moment_hbm.1), custom_call_target="tpu_custom_call" | custom-call | tf_op jit(solution)/shard_map/pallas_call | solution.py:522

commit v4 on v3

--- a/solution.py
+++ b/solution.py
@@ -21,6 +21,7 @@
 COLS = 256
 HALF = 256
 CHUNKS = 2
+PIECES = 2
 N_SLOTS = 124
 EXTRA = 32
 X_ROWS = (HALF, HALF)
@@ -30,45 +31,45 @@
 F32 = jnp.float32
 BF16 = jnp.bfloat16
 PLAN = (
-    ("gs", 0), ("fx", 0), ("gc", 0), ("gp", 0, 0),
-    ("gf", 0, 1, "o", 1), ("gf", 0, 1, "o", -1), ("enc",), ("fx", 1),
-    ("gf", 0, 1, "x", 1), ("gf", 0, 1, "x", -1), ("gf", 0, 1, "n", 1), ("gf", 0, 1, "n", -1),
-    ("gp", 0, 1), ("fx", 2), ("par",), ("gf", 0, 2, "o", 1),
-    ("gf", 0, 2, "o", -1), ("gf", 0, 2, "x", 1), ("gf", 0, 2, "x", -1), ("fx", 3),
-    ("dec",), ("gf", 0, 2, "n", 1), ("gf", 0, 2, "n", -1), ("gp", 0, 2),
-    ("gf", 0, 3, "o", 1), ("gf", 0, 3, "o", -1), ("fx", 4), ("upd",),
-    ("gf", 0, 3, "x", 1), ("gf", 0, 3, "x", -1), ("fx", 5), ("gf", 0, 3, "n", 1),
-    ("gf", 0, 3, "n", -1), ("gp", 0, 3), ("gs", 1), ("gf", 0, 4, "o", 1),
-    ("gf", 0, 4, "o", -1), ("gf", 0, 4, "x", 1), ("gf", 0, 4, "x", -1), ("gf", 0, 4, "n", 1),
-    ("gf", 0, 4, "n", -1), ("gp", 0, 4), ("gf", 1, 1, "o", 1), ("gf", 1, 1, "o", -1),
+    ("gs", 0), ("gb", 0), ("fx", 0), ("gc", 0),
+    ("gp", 0, 0), ("gf", 0, 1, "o", -1), ("gf", 0, 1, "o", 1), ("enc",),
+    ("fx", 1), ("gf", 0, 1, "x", 1), ("gf", 0, 1, "x", -1), ("gf", 0, 1, "n", 1),
+    ("gf", 0, 1, "n", -1), ("gp", 0, 1), ("fx", 2), ("par",),
+    ("gf", 0, 2, "o", 1), ("gf", 0, 2, "o", -1), ("gf", 0, 2, "x", 1), ("gf", 0, 2, "x", -1),
+    ("fx", 3), ("dec",), ("gf", 0, 2, "n", -1), ("gf", 0, 2, "n", 1),
+    ("gp", 0, 2), ("gf", 0, 3, "o", 1), ("gf", 0, 3, "o", -1), ("fx", 4),
+    ("gs", 1), ("upd",), ("gf", 0, 3, "x", -1), ("gf", 0, 3, "x", 1),
+    ("gf", 0, 3, "n", 1), ("gf", 0, 3, "n", -1), ("gp", 0, 3), ("gf", 0, 4, "o", 1),
+    ("gf", 0, 4, "o", -1), ("gb", 1), ("fx", 5), ("gf", 1, 1, "o", 1),
+    ("gf", 1, 1, "o", -1), ("gf", 0, 4, "x", 1), ("gf", 0, 4, "x", -1), ("gf", 0, 4, "n", 1),
+    ("gf", 0, 4, "n", -1), ("gp", 0, 4), ("gc", 1), ("gp", 1, 0),
     ("fx", 6), ("gf", 1, 1, "x", 1), ("gf", 1, 1, "x", -1), ("gf", 1, 2, "o", 1),
-    ("gf", 1, 2, "o", -1), ("gc", 1), ("gp", 1, 0), ("fx", 7),
-    ("gf", 1, 2, "x", 1), ("gf", 1, 2, "x", -1), ("gf", 1, 3, "o", 1), ("gf", 1, 3, "o", -1),
-    ("gf", 1, 1, "n", 1), ("gf", 1, 1, "n", -1), ("gp", 1, 1), ("gq", 0, 0),
-    ("gq", 0, 1), ("gf", 1, 3, "x", 1), ("gf", 1, 3, "x", -1), ("gq", 0, 2),
+    ("gf", 1, 2, "o", -1), ("fx", 7), ("gf", 1, 1, "n", 1), ("gf", 1, 1, "n", -1),
+    ("gp", 1, 1), ("gf", 1, 2, "x", 1), ("gf", 1, 2, "x", -1), ("gf", 1, 3, "o", 1),
+    ("gf", 1, 3, "o", -1), ("gq", 0, 0), ("gq", 0, 1), ("gq", 0, 2),
     ("gq", 0, 3), ("gq", 0, 4), ("gq", 1, 0), ("gq", 1, 1),
-    ("gf", 1, 4, "o", 1), ("gf", 1, 4, "o", -1), ("gf", 1, 2, "n", 1), ("gf", 1, 2, "n", -1),
-    ("gp", 1, 2), ("gq", 1, 2), ("gf", 1, 4, "x", 1), ("gf", 1, 4, "x", -1),
-    ("sc", 0), ("ss", 0), ("rf", 0, "o"), ("rf", 0, "n"),
-    ("gf", 1, 3, "n", 1), ("gf", 1, 3, "n", -1), ("gp", 1, 3), ("gq", 1, 3),
-    ("rc", 0, 0), ("rc", 0, 1), ("rs", 0, 1, "o", 1), ("rs", 0, 1, "o", -1),
-    ("rc", 0, 2), ("rs", 0, 1, "n", 1), ("rs", 0, 1, "n", -1), ("rc", 0, 3),
-    ("rc", 0, 4), ("gf", 1, 4, "n", 1), ("rc", 0, 5), ("gf", 1, 4, "n", -1),
-    ("gp", 1, 4), ("gq", 1, 4), ("rf", 0, "b"), ("rs", 0, 2, "o", 1),
-    ("rs", 0, 2, "o", -1), ("rf", 0, "x"), ("rs", 0, 2, "n", 1), ("rs", 0, 2, "n", -1),
-    ("rs", 0, 1, "b", 1), ("rs", 0, 1, "b", -1), ("rc", 0, 6), ("rc", 0, 7),
-    ("rs", 0, 3, "o", 1), ("rs", 0, 3, "o", -1), ("rs", 0, 1, "x", 1), ("rs", 0, 1, "x", -1),
-    ("rs", 0, 3, "n", 1), ("rs", 0, 3, "n", -1), ("sc", 1), ("ss", 1),
-    ("rs", 0, 2, "b", 1), ("rs", 0, 2, "b", -1), ("rc", 1, 0), ("rl", 0, "o"),
-    ("rs", 0, 2, "x", 1), ("rs", 0, 2, "x", -1), ("rc", 1, 1), ("rl", 0, "n"),
-    ("rf", 1, "b"), ("rs", 0, 3, "b", 1), ("rs", 0, 3, "b", -1), ("rc", 1, 2),
-    ("rs", 0, 3, "x", 1), ("rs", 0, 3, "x", -1), ("rf", 1, "x"), ("rs", 1, 1, "b", 1),
-    ("rs", 1, 1, "b", -1), ("rc", 1, 3), ("rl", 0, "b"), ("rc", 1, 4),
-    ("rl", 0, "x"), ("fin", 0), ("rs", 1, 1, "x", 1), ("rs", 1, 1, "x", -1),
-    ("rc", 1, 5), ("rs", 1, 2, "b", 1), ("rs", 1, 2, "b", -1), ("rc", 1, 6),
-    ("rs", 1, 2, "x", 1), ("rs", 1, 2, "x", -1), ("rc", 1, 7), ("rs", 1, 3, "b", 1),
-    ("rs", 1, 3, "b", -1), ("rs", 1, 3, "x", 1), ("rs", 1, 3, "x", -1), ("rl", 1, "b"),
-    ("rl", 1, "x"), ("fin", 1),
+    ("gq", 1, 2), ("gf", 1, 2, "n", -1), ("gf", 1, 2, "n", 1), ("gp", 1, 2),
+    ("gf", 1, 3, "x", 1), ("gf", 1, 3, "x", -1), ("gq", 1, 3), ("gf", 1, 4, "o", 1),
+    ("gf", 1, 4, "o", -1), ("gf", 1, 3, "n", 1), ("gf", 1, 3, "n", -1), ("gp", 1, 3),
+    ("sc", 0), ("ss", 0), ("rf", 0, "n"), ("gf", 1, 4, "x", -1),
+    ("gf", 1, 4, "x", 1), ("gq", 1, 4), ("rf", 0, "o"), ("gf", 1, 4, "n", 1),
+    ("gf", 1, 4, "n", -1), ("gp", 1, 4), ("rs", 0, 1, "n", 1), ("rs", 0, 1, "n", -1),
+    ("rs", 0, 1, "o", 1), ("rs", 0, 1, "o", -1), ("rf", 0, "b"), ("rs", 0, 2, "n", 1),
+    ("rs", 0, 2, "n", -1), ("rc", 0, 0), ("rc", 0, 1), ("rs", 0, 2, "o", 1),
+    ("rs", 0, 2, "o", -1), ("rc", 0, 2), ("rc", 0, 3), ("rs", 0, 1, "b", 1),
+    ("rs", 0, 1, "b", -1), ("rc", 0, 4), ("rc", 0, 5), ("sc", 1),
+    ("rc", 0, 6), ("ss", 1), ("rs", 0, 3, "n", 1), ("rs", 0, 3, "n", -1),
+    ("rf", 0, "x"), ("rs", 0, 3, "o", 1), ("rs", 0, 3, "o", -1), ("rs", 0, 2, "b", 1),
+    ("rs", 0, 2, "b", -1), ("rc", 1, 0), ("rl", 0, "n"), ("rs", 0, 1, "x", -1),
+    ("rs", 0, 1, "x", 1), ("rf", 1, "b"), ("rl", 0, "o"), ("rc", 1, 1),
+    ("rf", 1, "x"), ("rs", 0, 3, "b", 1), ("rs", 0, 3, "b", -1), ("rc", 1, 2),
+    ("rs", 0, 2, "x", 1), ("rs", 0, 2, "x", -1), ("rs", 1, 1, "b", 1), ("rs", 1, 1, "b", -1),
+    ("rc", 1, 3), ("rs", 1, 1, "x", 1), ("rc", 1, 4), ("rl", 0, "b"),
+    ("rs", 0, 3, "x", 1), ("rs", 0, 3, "x", -1), ("rs", 1, 1, "x", -1), ("rc", 1, 5),
+    ("rs", 1, 2, "b", 1), ("rs", 1, 2, "b", -1), ("rc", 1, 6), ("rs", 1, 2, "x", 1),
+    ("rs", 1, 2, "x", -1), ("rc", 1, 7), ("rs", 1, 3, "b", 1), ("rs", 1, 3, "b", -1),
+    ("rc", 0, 7), ("rs", 1, 3, "x", 1), ("rs", 1, 3, "x", -1), ("rl", 0, "x"),
+    ("fin", 0), ("rl", 1, "b"), ("rl", 1, "x"), ("fin", 1),
 )
 
 
@@ -175,16 +176,17 @@
         return (lo, n // 2) if d == 1 else (lo + n // 2, n // 2)
 
     def gather_start(c):
-        loads[f"w{c}"].wait()
-        own = blk(0, 0)
+        loads_once(f"w{c}")
         lo, n = gather_span(c, "o")
-        if n:
-            gather_push(("nb", c), c, own, lo, n, xdev)
-        for name in ("o", "x"):
-            lo, n = gather_span(c, name)
-            if n:
-                for d in (1, -1):
-                    gather_push(("g", c, d, 1, name), c, own, lo, n, zdev[d])
+        gather_push(("nb", c), c, blk(0, 0), lo, n, xdev)
+        for d in (1, -1):
+            gather_push(("g", c, d, 1, "o"), c, blk(0, 0), lo, n, zdev[d])
+
+    def gather_half(c):
+        loads_once(f"w{c}")
+        lo, n = gather_span(c, "x")
+        for d in (1, -1):
+            gather_push(("g", c, d, 1, "x"), c, blk(0, 0), lo, n, zdev[d])
 
     def gather_cross(c):
         lo, n = gather_span(c, "n")
@@ -403,6 +405,7 @@
 
     steps = {
         "gs": gather_start,
+        "gb": gather_half,
         "gc": gather_cross,
         "gf": gather_forward,
         "gp": product,
@@ -437,12 +440,13 @@
 
 
 def finish_kernel(gt_hbm, delta_hbm, params_hbm, moment_hbm, grad_hbm, newp_hbm, newm_hbm, gt, dlt, params, moment, out, newp, newm, load_sem, store_sem):
+    piece = BLK // PIECES
     loads = [
-        pltpu.make_async_copy(gt_hbm.at[c], gt.at[c], load_sem.at[c]) for c in range(CHUNKS)
+        pltpu.make_async_copy(gt_hbm.at[:, :, pl.ds(q * piece, piece)], gt.at[q], load_sem.at[q]) for q in range(PIECES)
     ] + [
-        pltpu.make_async_copy(delta_hbm, dlt, load_sem.at[CHUNKS]),
-        pltpu.make_async_copy(params_hbm, params, load_sem.at[CHUNKS + 1]),
-        pltpu.make_async_copy(moment_hbm, moment, load_sem.at[CHUNKS + 2]),
+        pltpu.make_async_copy(delta_hbm, dlt, load_sem.at[PIECES]),
+        pltpu.make_async_copy(params_hbm, params, load_sem.at[PIECES + 1]),
+        pltpu.make_async_copy(moment_hbm, moment, load_sem.at[PIECES + 2]),
     ]
     for copy in loads:
         copy.start()
@@ -453,11 +457,12 @@
         copy.start()
         stores.append(copy)
 
-    for c in range(CHUNKS):
-        loads[c].wait()
-        out[:, c * COLS : (c + 1) * COLS] = gt[c].T
-    store(out, grad_hbm.at[0])
-    for copy in loads[CHUNKS:]:
+    for q in range(PIECES):
+        loads[q].wait()
+        for c in range(CHUNKS):
+            out[q * piece : (q + 1) * piece, c * COLS : (c + 1) * COLS] = gt[q, c].T
+        store(out.at[pl.ds(q * piece, piece)], grad_hbm.at[0, pl.ds(q * piece, piece)])
+    for copy in loads[PIECES:]:
         copy.wait()
     delta = dlt[...].astype(F32)
     new = MOMENTUM * moment[...] + delta
@@ -529,15 +534,15 @@
         in_specs=[hbm] * 4,
         out_specs=(hbm,) * 3,
         scratch_shapes=[
-            pltpu.VMEM((CHUNKS, COLS, BLK), F32),
+            pltpu.VMEM((PIECES, CHUNKS, COLS, BLK // PIECES), F32),
             pltpu.VMEM((16, WIDTH), BF16),
             wide,
             wide,
             pltpu.VMEM((BLK, CHUNKS * COLS), F32),
             wide,
             wide,
-            pltpu.SemaphoreType.DMA((CHUNKS + 3,)),
-            pltpu.SemaphoreType.DMA((3,)),
+            pltpu.SemaphoreType.DMA((PIECES + 3,)),
+            pltpu.SemaphoreType.DMA((PIECES + 2,)),
         ],
         compiler_params=pltpu.CompilerParams(vmem_limit_bytes=60 * 2**20),
     )(*out, outer_params, outer_moment)

time: 127 us -> 127 us (level)
  no operation moved by 1% of the time
where the time goes in v4:
time: 127 us; the launch traced here: 126 us
  Pallas kernels  126 us (99%)
    pallas_call x1, Pallas kernels, on_device(): pl.pallas_call(kernel, out_shape=(jax.ShapeDtypeStruct((CHUNKS, COLS, BLK...  123 us
    pallas_call x1, Pallas kernels, on_device(): pl.pallas_call(finish_kernel, out_shape=(jax.ShapeDtypeStruct((1, BLK, CH...  2.73 us

profile of v4, /device:TPU:2, one launch (start us, length us, event | category | flops | bytes accessed | tf_op | source)
XLA Modules:
  0.0 126.4 jit_solution(7870163435491319652)
XLA Ops:
  0.6 122.9 %shard_map.112 = (f32[2,256,512]{2,1,0:T(8,128)}, bf16[16,8192]{1,0:T(8,128)(2,1)}) custom-call(bf16[1,512,8192]{2,1,0:T(8,128)(2,1)} %feats_hbm.1, bf16[1,512,512]{2,1,0:T(8,128)(2,1)} %targs_hbm.1, bf16[1,512,512]{2,1,0:T(8,128)(2,1)} %weight_hbm.1, s32[1,512]{1,0:T(1,128)} %seg_hbm.1, s32[1,8]{1,0:T(1,128)} %counts_hbm.1, f32[1,16,8192]{2,1,0:T(8,128)} %pg_hbm.1, ...), custom_call_target="tpu_custom_call" | custom-call | tf_op jit(solution)/shard_map/pallas_call | solution.py:481
  123.6 2.7 %shard_map.113 = (f32[1,512,512]{2,1,0:T(8,128)}, f32[16,8192]{1,0:T(8,128)}, f32[16,8192]{1,0:T(8,128)}) custom-call(f32[2,256,512]{2,1,0:T(8,128)} %get-tuple-element.5.gt_hbm, bf16[16,8192]{1,0:T(8,128)(2,1)} %get-tuple-element.6.delta_hbm, f32[16,8192]{1,0:T(8,128)} %params_hbm.1, f32[16,8192]{1,0:T(8,128)} %moment_hbm.1), custom_call_target="tpu_custom_call" | custom-call | tf_op jit(solution)/shard_map/pallas_call | solution.py:527

commit v5 on v3

--- a/solution.py
+++ b/solution.py
@@ -37,34 +37,34 @@
     ("gf", 0, 2, "o", -1), ("gf", 0, 2, "x", 1), ("gf", 0, 2, "x", -1), ("fx", 3),
     ("dec",), ("gf", 0, 2, "n", 1), ("gf", 0, 2, "n", -1), ("gp", 0, 2),
     ("gf", 0, 3, "o", 1), ("gf", 0, 3, "o", -1), ("fx", 4), ("upd",),
-    ("gf", 0, 3, "x", 1), ("gf", 0, 3, "x", -1), ("fx", 5), ("gf", 0, 3, "n", 1),
-    ("gf", 0, 3, "n", -1), ("gp", 0, 3), ("gs", 1), ("gf", 0, 4, "o", 1),
+    ("gf", 0, 3, "x", 1), ("gf", 0, 3, "x", -1), ("gf", 0, 3, "n", 1), ("gf", 0, 3, "n", -1),
+    ("gp", 0, 3), ("fx", 5), ("gs", 1), ("gf", 0, 4, "o", 1),
     ("gf", 0, 4, "o", -1), ("gf", 0, 4, "x", 1), ("gf", 0, 4, "x", -1), ("gf", 0, 4, "n", 1),
     ("gf", 0, 4, "n", -1), ("gp", 0, 4), ("gf", 1, 1, "o", 1), ("gf", 1, 1, "o", -1),
-    ("fx", 6), ("gf", 1, 1, "x", 1), ("gf", 1, 1, "x", -1), ("gf", 1, 2, "o", 1),
-    ("gf", 1, 2, "o", -1), ("gc", 1), ("gp", 1, 0), ("fx", 7),
-    ("gf", 1, 2, "x", 1), ("gf", 1, 2, "x", -1), ("gf", 1, 3, "o", 1), ("gf", 1, 3, "o", -1),
-    ("gf", 1, 1, "n", 1), ("gf", 1, 1, "n", -1), ("gp", 1, 1), ("gq", 0, 0),
-    ("gq", 0, 1), ("gf", 1, 3, "x", 1), ("gf", 1, 3, "x", -1), ("gq", 0, 2),
-    ("gq", 0, 3), ("gq", 0, 4), ("gq", 1, 0), ("gq", 1, 1),
-    ("gf", 1, 4, "o", 1), ("gf", 1, 4, "o", -1), ("gf", 1, 2, "n", 1), ("gf", 1, 2, "n", -1),
-    ("gp", 1, 2), ("gq", 1, 2), ("gf", 1, 4, "x", 1), ("gf", 1, 4, "x", -1),
+    ("fx", 6), ("gf", 1, 1, "x", 1), ("gf", 1, 1, "x", -1), ("gc", 1),
+    ("gp", 1, 0), ("gf", 1, 2, "o", 1), ("gf", 1, 2, "o", -1), ("fx", 7),
+    ("gf", 1, 2, "x", 1), ("gf", 1, 2, "x", -1), ("gf", 1, 1, "n", 1), ("gf", 1, 1, "n", -1),
+    ("gp", 1, 1), ("gf", 1, 3, "o", 1), ("gf", 1, 3, "o", -1), ("gq", 0, 0),
+    ("gq", 0, 1), ("gq", 0, 2), ("gq", 0, 3), ("gq", 0, 4),
+    ("gq", 1, 0), ("gf", 1, 3, "x", 1), ("gf", 1, 3, "x", -1), ("gq", 1, 1),
+    ("gf", 1, 2, "n", 1), ("gf", 1, 2, "n", -1), ("gp", 1, 2), ("gq", 1, 2),
+    ("gf", 1, 4, "o", 1), ("gf", 1, 4, "o", -1), ("gf", 1, 4, "x", 1), ("gf", 1, 4, "x", -1),
     ("sc", 0), ("ss", 0), ("rf", 0, "o"), ("rf", 0, "n"),
     ("gf", 1, 3, "n", 1), ("gf", 1, 3, "n", -1), ("gp", 1, 3), ("gq", 1, 3),
-    ("rc", 0, 0), ("rc", 0, 1), ("rs", 0, 1, "o", 1), ("rs", 0, 1, "o", -1),
-    ("rc", 0, 2), ("rs", 0, 1, "n", 1), ("rs", 0, 1, "n", -1), ("rc", 0, 3),
-    ("rc", 0, 4), ("gf", 1, 4, "n", 1), ("rc", 0, 5), ("gf", 1, 4, "n", -1),
-    ("gp", 1, 4), ("gq", 1, 4), ("rf", 0, "b"), ("rs", 0, 2, "o", 1),
-    ("rs", 0, 2, "o", -1), ("rf", 0, "x"), ("rs", 0, 2, "n", 1), ("rs", 0, 2, "n", -1),
-    ("rs", 0, 1, "b", 1), ("rs", 0, 1, "b", -1), ("rc", 0, 6), ("rc", 0, 7),
+    ("rs", 0, 1, "o", 1), ("rs", 0, 1, "o", -1), ("rc", 0, 0), ("rc", 0, 1),
+    ("rs", 0, 1, "n", 1), ("rs", 0, 1, "n", -1), ("rc", 0, 2), ("rc", 0, 3),
+    ("gf", 1, 4, "n", 1), ("gf", 1, 4, "n", -1), ("gp", 1, 4), ("gq", 1, 4),
+    ("rf", 0, "b"), ("rs", 0, 2, "o", 1), ("rs", 0, 2, "o", -1), ("rf", 0, "x"),
+    ("rs", 0, 2, "n", 1), ("rs", 0, 2, "n", -1), ("rs", 0, 1, "b", 1), ("rs", 0, 1, "b", -1),
+    ("rc", 0, 4), ("rc", 0, 5), ("rc", 0, 6), ("rc", 0, 7),
     ("rs", 0, 3, "o", 1), ("rs", 0, 3, "o", -1), ("rs", 0, 1, "x", 1), ("rs", 0, 1, "x", -1),
-    ("rs", 0, 3, "n", 1), ("rs", 0, 3, "n", -1), ("sc", 1), ("ss", 1),
+    ("sc", 1), ("ss", 1), ("rs", 0, 3, "n", 1), ("rs", 0, 3, "n", -1),
     ("rs", 0, 2, "b", 1), ("rs", 0, 2, "b", -1), ("rc", 1, 0), ("rl", 0, "o"),
-    ("rs", 0, 2, "x", 1), ("rs", 0, 2, "x", -1), ("rc", 1, 1), ("rl", 0, "n"),
-    ("rf", 1, "b"), ("rs", 0, 3, "b", 1), ("rs", 0, 3, "b", -1), ("rc", 1, 2),
-    ("rs", 0, 3, "x", 1), ("rs", 0, 3, "x", -1), ("rf", 1, "x"), ("rs", 1, 1, "b", 1),
-    ("rs", 1, 1, "b", -1), ("rc", 1, 3), ("rl", 0, "b"), ("rc", 1, 4),
-    ("rl", 0, "x"), ("fin", 0), ("rs", 1, 1, "x", 1), ("rs", 1, 1, "x", -1),
+    ("rs", 0, 2, "x", 1), ("rs", 0, 2, "x", -1), ("rc", 1, 1), ("rf", 1, "b"),
+    ("rl", 0, "n"), ("rf", 1, "x"), ("rs", 0, 3, "b", 1), ("rs", 0, 3, "b", -1),
+    ("rc", 1, 2), ("rs", 0, 3, "x", 1), ("rs", 0, 3, "x", -1), ("rs", 1, 1, "b", 1),
+    ("rs", 1, 1, "b", -1), ("rc", 1, 3), ("rs", 1, 1, "x", 1), ("rc", 1, 4),
+    ("rl", 0, "b"), ("rs", 1, 1, "x", -1), ("rl", 0, "x"), ("fin", 0),
     ("rc", 1, 5), ("rs", 1, 2, "b", 1), ("rs", 1, 2, "b", -1), ("rc", 1, 6),
     ("rs", 1, 2, "x", 1), ("rs", 1, 2, "x", -1), ("rc", 1, 7), ("rs", 1, 3, "b", 1),
     ("rs", 1, 3, "b", -1), ("rs", 1, 3, "x", 1), ("rs", 1, 3, "x", -1), ("rl", 1, "b"),
@@ -216,9 +216,8 @@
                     acc[c] += part
 
     def lend(ki):
-        loads_once("feats")
         cols = pl.ds(pl.multiple_of(blk(1, ORDER[ki]) * BLK, BLK), HALF)
-        send(("fx", ki), feats.at[:, cols], fnb.at[ki], xdev, 9)
+        send(("fx", ki), feats_hbm.at[0, :, cols], fnb.at[ki], xdev, 9)
 
     def product_lent(c, k):
         for kk in (k,) if k in (0, 4) else (k, -k):

time: 127 us -> 127 us (level)
  no operation moved by 1% of the time
where the time goes in v5:
time: 127 us
  Pallas kernels  126 us (99%)
    pallas_call x1, Pallas kernels, on_device(): pl.pallas_call(kernel, out_shape=(jax.ShapeDtypeStruct((CHUNKS, COLS, BLK...  123 us
    pallas_call x1, Pallas kernels, on_device(): pl.pallas_call(finish_kernel, out_shape=(jax.ShapeDtypeStruct((1, BLK, CH...  2.83 us

profile of v5, /device:TPU:2, one launch (start us, length us, event | category | flops | bytes accessed | tf_op | source)
XLA Modules:
  0.0 126.9 jit_solution(5258862359009449435)
XLA Ops:
  0.6 123.3 %shard_map.112 = (f32[2,256,512]{2,1,0:T(8,128)}, bf16[16,8192]{1,0:T(8,128)(2,1)}) custom-call(bf16[1,512,8192]{2,1,0:T(8,128)(2,1)} %feats_hbm.1, bf16[1,512,512]{2,1,0:T(8,128)(2,1)} %targs_hbm.1, bf16[1,512,512]{2,1,0:T(8,128)(2,1)} %weight_hbm.1, s32[1,512]{1,0:T(1,128)} %seg_hbm.1, s32[1,8]{1,0:T(1,128)} %counts_hbm.1, f32[1,16,8192]{2,1,0:T(8,128)} %pg_hbm.1, ...), custom_call_target="tpu_custom_call" | custom-call | tf_op jit(solution)/shard_map/pallas_call | solution.py:475
  123.9 2.8 %shard_map.113 = (f32[1,512,512]{2,1,0:T(8,128)}, f32[16,8192]{1,0:T(8,128)}, f32[16,8192]{1,0:T(8,128)}) custom-call(f32[2,256,512]{2,1,0:T(8,128)} %get-tuple-element.5.gt_hbm, bf16[16,8192]{1,0:T(8,128)(2,1)} %get-tuple-element.6.delta_hbm, f32[16,8192]{1,0:T(8,128)} %params_hbm.1, f32[16,8192]{1,0:T(8,128)} %moment_hbm.1), custom_call_target="tpu_custom_call" | custom-call | tf_op jit(solution)/shard_map/pallas_call | solution.py:521
